TPU v7x, 256 devices: a whole 4x4x8 slice. The times are simulated.
256 devices in a mesh: lon: 32 (over x, y, z_lo), lat: 8 (over z_hi, core).
Axes of the slice: x: 4, y: 4, z: 8 (z_hi: 4, z_lo: 2; z = z_hi * 2 + z_lo), core: 2. Of those that a mesh axis runs over, the one named last changes fastest.
Arguments:
- thermal_field: float32 [128, 16, 16384], P(None, 'lat', 'lon'), may hold values from -6 to 6
- zonal_weights: float32 [2, 16, 16384], P(None, 'lat', 'lon'), may hold values from 0.05 to 0.3
- meridional_weights: float32 [2, 16, 16384], P(None, 'lat', 'lon'), may hold values from 0.02 to 0.1
- gas_burden: bfloat16 [16, 16384, 2048], P('lat', 'lon'), may hold values from 0.5 to 2
- tier_air_weight: bfloat16 [16, 16384, 128], P('lat', 'lon'), may hold values from 0.5 to 2
- solar_elevation_factor: bfloat16 [16, 16384], P('lat', 'lon'), may hold values from 0.099609375 to 1
- ground_reflectance: bfloat16 [16, 16384], P('lat', 'lon'), may hold values from 0.049804688 to 0.8984375
- extinction_table: float32 [16, 224], replicated, may hold values from 2e-05 to 0.004
- incoming_irradiance: float32 [224], replicated, may hold values from 0.1 to 3
- daytime_tile_tally: int32 [8, 32], P('lat', 'lon'), may hold values from 1 to 256, 4096 in all within a row
- daytime_tile_order: int32 [8, 32, 256], P('lat', 'lon'), may hold values from 0 to 255, each once within a row
Outputs:
- temperature_next: float32 [128, 16, 16384], P(None, 'lat', 'lon')
Inputs may be any that keep to these rules, and one draw needn't show every extreme that they name: `daytime_tile_tally`: in each latitude band the counts of the 32 devices sum to 4096, and some device of the band has all 256 blocks daylit. `daytime_tile_order`: each device's list names each of its 256 blocks once.
All inputs are finite; a program needn't handle non-finite values.
Results may differ from a plain program's by a relative error of at most 0.0006.
Values may be sent and summed in bfloat16 or wider, within the bound.
No kernel may reach another device: no remote copies, remote signals or barrier semaphores. Data moves between devices by JAX's collectives and lax.ppermute only.
A program may use at most 128 MiB of HBM per device.

v0:
```python
import jax
import jax.numpy as jnp
from jax import lax
from jax.sharding import PartitionSpec as P

DSTEPS = 2


DIFFUSE = 1.66


def padded(cells, sides, width, closed):
    for axis, dim in sides:
        count = lax.axis_size(axis)
        ends = count if closed else count - 1
        head = lax.slice_in_dim(cells, 0, width, axis=dim)
        tail = lax.slice_in_dim(cells, cells.shape[dim] - width, cells.shape[dim], axis=dim)
        cells = jnp.concatenate(
            [
                lax.ppermute(tail, axis, [(i, (i + 1) % count) for i in range(ends)]),
                cells,
                lax.ppermute(head, axis, [((i + 1) % count, i) for i in range(ends)]),
            ],
            axis=dim,
        )
    return cells


def entering(part, axis, combine, identity):
    place = lax.axis_index(axis)
    gathered = lax.all_gather(part, axis)
    state = jnp.zeros_like(part) + jnp.asarray(identity, part.dtype)

    def one(turn, state):
        return combine(state, lax.dynamic_index_in_dim(gathered, turn, 0, False))

    return lax.fori_loop(0, place, one, state)


def column_heating(
    gas_burden,
    tier_air_weight,
    solar_elevation_factor,
    ground_reflectance,
    extinction_table,
    incoming_irradiance,
):
    columns = gas_burden.shape[0]
    tier_number = tier_air_weight.shape[1]
    gases = extinction_table.shape[0]
    amounts = gas_burden.astype(jnp.float32).reshape(columns, tier_number, gases)
    summed = jnp.cumsum(amounts, axis=1)
    column_above = jnp.concatenate([jnp.zeros((columns, 1, gases), jnp.float32), summed], axis=1)
    optical_depth = jnp.einsum(
        "cij,jg->cig", column_above, extinction_table, precision=lax.Precision.HIGHEST
    )
    cosine_col = solar_elevation_factor.astype(jnp.float32)[:, None, None]
    downward = (
        incoming_irradiance[None, None, :] * cosine_col * jnp.exp(-optical_depth / cosine_col)
    )
    upward = (
        ground_reflectance.astype(jnp.float32)[:, None, None]
        * downward[:, -1:, :]
        * jnp.exp(-DIFFUSE * (optical_depth[:, -1:, :] - optical_depth))
    )
    net_flux = jnp.sum(downward - upward, axis=2)
    return (net_flux[:, :-1] - net_flux[:, 1:]) / tier_air_weight.astype(jnp.float32)


def heating_groups(
    gas_burden,
    tier_air_weight,
    solar_elevation_factor,
    ground_reflectance,
    extinction_table,
    incoming_irradiance,
):
    columns = gas_burden.shape[0]
    tier_number = tier_air_weight.shape[1]
    group_size = 128
    group_count = columns // group_size

    def one_group(pieces):
        return column_heating(
            pieces[0], pieces[1], pieces[2], pieces[3], extinction_table, incoming_irradiance
        )

    result = lax.map(
        one_group,
        (
            gas_burden.reshape(group_count, group_size, gas_burden.shape[1]),
            tier_air_weight.reshape(group_count, group_size, tier_number),
            solar_elevation_factor.reshape(group_count, group_size),
            ground_reflectance.reshape(group_count, group_size),
        ),
    )
    return result.reshape(columns, tier_number)


def march_forward(thermal_field, zonal_weights, meridional_weights):
    prognostic_field = thermal_field
    for step_index in range(DSTEPS):
        lon_rims = padded(prognostic_field, (("lon", 2),), 1, True)
        lat_rims = padded(prognostic_field.astype(jnp.bfloat16), (("lat", 1),), 1, False).astype(
            prognostic_field.dtype
        )
        western = lon_rims[:, :, :-2]
        eastern = lon_rims[:, :, 2:]
        southern = lat_rims[:, :-2, :]
        northern = lat_rims[:, 2:, :]
        prognostic_field = (
            prognostic_field
            + zonal_weights[0] * (western - prognostic_field)
            + zonal_weights[1] * (eastern - prognostic_field)
            + meridional_weights[0] * (southern - prognostic_field)
            + meridional_weights[1] * (northern - prognostic_field)
        )
    return prognostic_field


def add_counts(earlier, later):
    return earlier + later


def compute_filled(
    arrived,
    slot_total,
    take_count,
    block_width,
    features,
    tier_number,
    extinction_table,
    incoming_irradiance,
):
    filled = arrived[4].reshape(slot_total) > 0.5
    sort_keys = jnp.where(filled, 0, slot_total) + jnp.arange(slot_total, dtype=jnp.int32)
    chosen = jnp.argsort(sort_keys)[:take_count]
    computed = heating_groups(
        arrived[0]
        .reshape(slot_total, block_width, features)[chosen]
        .reshape(take_count * block_width, features),
        arrived[1]
        .reshape(slot_total, block_width, tier_number)[chosen]
        .reshape(take_count * block_width, tier_number),
        arrived[2].reshape(slot_total, block_width)[chosen].reshape(take_count * block_width),
        arrived[3].reshape(slot_total, block_width)[chosen].reshape(take_count * block_width),
        extinction_table,
        incoming_irradiance,
    )
    computed = jnp.where(
        filled[chosen][:, None, None], computed.reshape(take_count, block_width, tier_number), 0.0
    )
    return jnp.zeros((slot_total, block_width, tier_number), jnp.float32).at[chosen].set(computed)


def per_device(
    thermal_field,
    zonal_weights,
    meridional_weights,
    gas_burden,
    tier_air_weight,
    solar_elevation_factor,
    ground_reflectance,
    extinction_table,
    incoming_irradiance,
    daytime_tile_tally,
    daytime_tile_order,
):
    prognostic_field = march_forward(thermal_field, zonal_weights, meridional_weights)
    tier_number, meridian_stripes, zonal_point_number = thermal_field.shape
    block_count = daytime_tile_order.shape[2]
    block_width = meridian_stripes * zonal_point_number // block_count
    features = gas_burden.shape[2]
    own_count = daytime_tile_tally[0, 0]
    own_order = daytime_tile_order[0, 0]
    block_abs = gas_burden.reshape(block_count, block_width, features)
    block_mass = tier_air_weight.reshape(block_count, block_width, tier_number)
    block_cos = solar_elevation_factor.reshape(block_count, block_width)
    block_alb = ground_reflectance.reshape(block_count, block_width)
    lon_count = lax.axis_size("lon")
    half_blocks = block_count // 2
    capacity = (block_count + lon_count - 1) // lon_count
    offset = entering(own_count.reshape(1), "lon", add_counts, jnp.zeros((1,), jnp.int32))[0]
    targets = jnp.arange(lon_count, dtype=jnp.int32)[:, None]
    slot_index = jnp.arange(capacity, dtype=jnp.int32)[None, :]
    ordinal = slot_index * lon_count + jnp.mod(targets - offset, lon_count)
    active = ordinal < own_count
    picked = own_order[jnp.minimum(ordinal, block_count - 1)]
    arrived = (
        lax.all_to_all(block_abs[picked], "lon", split_axis=0, concat_axis=0, tiled=True),
        lax.all_to_all(block_mass[picked], "lon", split_axis=0, concat_axis=0, tiled=True),
        lax.all_to_all(block_cos[picked], "lon", split_axis=0, concat_axis=0, tiled=True),
        lax.all_to_all(block_alb[picked], "lon", split_axis=0, concat_axis=0, tiled=True),
        lax.all_to_all(active.astype(jnp.bfloat16), "lon", split_axis=0, concat_axis=0, tiled=True),
    )
    slot_total = lon_count * capacity
    replies = compute_filled(
        arrived,
        slot_total,
        half_blocks,
        block_width,
        features,
        tier_number,
        extinction_table,
        incoming_irradiance,
    )
    returned = lax.all_to_all(
        replies.reshape(lon_count, capacity, block_width, tier_number),
        "lon",
        split_axis=0,
        concat_axis=0,
        tiled=True,
    )
    kept_heat = jnp.where(active[:, :, None, None], returned, 0.0)
    block_heat = (
        jnp.zeros((block_count, block_width, tier_number), jnp.float32)
        .at[picked.reshape(slot_total)]
        .add(kept_heat.reshape(slot_total, block_width, tier_number))
    )
    heat_map = block_heat.reshape(meridian_stripes, zonal_point_number, tier_number).transpose(
        2, 0, 1
    )
    return prognostic_field + heat_map


def solution(mesh):
    placed = (
        P(None, "lat", "lon"),
        P(None, "lat", "lon"),
        P(None, "lat", "lon"),
        P("lat", "lon", None),
        P("lat", "lon", None),
        P("lat", "lon"),
        P("lat", "lon"),
        P(),
        P(),
        P("lat", "lon"),
        P("lat", "lon", None),
    )
    return jax.shard_map(
        per_device, mesh=mesh, in_specs=placed, out_specs=P(None, "lat", "lon"), check_vma=False
    )
```

profile of v0, /device:TPU:65, one launch (start us, length us, event | category | flops | bytes accessed | tf_op | source)
XLA Modules:
  0.0 353.3 jit_solution(4981366447516899651)
XLA Ops:
  2.7 15.2 %all-reduce.1 = s32[32]{0:T(128)S(1)} all-reduce(s32[32]{0:T(128)S(1)} %bitcast_dynamic-update-slice_fusion), channel_id=1, replica_groups=mesh['lon'=32,'lat'=8] {'lon'}, use_global_device_ids=true, to_apply=%add.1 | all-reduce | flops 32 | bytes 256
  18.7 42.9 %all-to-all-start = ((bf16[32,1,8]{2,1,0:T(2,128)(2,1)}), bf16[32,1,8]{2,1,0:T(2,128)(2,1)S(1)}, u32[]{:S(2)}, u32[]{:S(2)}) async-start(bf16[32,1,8]{2,1,0:T(2,128)(2,1)} %copy.70), calls=%async_computation | async-start | bytes 32768 | tf_op jit(solution)/shard_map/all_to_all | solution.py:194
  65.8 2.8 all-to-all-done
  68.6 4.9 %all-to-all-start.1 = ((bf16[32,8,4]{1,2,0:T(4,128)(2,1)}), bf16[32,8,4]{1,2,0:T(4,128)(2,1)S(1)}, u32[]{:S(2)}, u32[]{:S(2)}) async-start(bf16[32,8,4]{1,2,0:T(4,128)(2,1)} %copy.71), calls=%async_computation.1 | async-start | bytes 65536 | tf_op jit(solution)/shard_map/all_to_all | solution.py:192
  75.5 5.2 %all-to-all-done.1 = bf16[32,8,4]{1,2,0:T(4,128)(2,1)S(1)} async-done(((bf16[32,8,4]{1,2,0:T(4,128)(2,1)}), bf16[32,8,4]{1,2,0:T(4,128)(2,1)S(1)}, u32[]{:S(2)}, u32[]{:S(2)}) %all-to-all-start.1) | async-done | bytes 2080 | tf_op jit(solution)/shard_map/all_to_all | solution.py:192
  80.7 3.8 %all-to-all-start.3 = ((bf16[32,8,4]{1,2,0:T(4,128)(2,1)}), bf16[32,8,4]{1,2,0:T(4,128)(2,1)S(1)}, u32[]{:S(2)}, u32[]{:S(2)}) async-start(bf16[32,8,4]{1,2,0:T(4,128)(2,1)} %copy.73), calls=%async_computation.3 | async-start | bytes 65536 | tf_op jit(solution)/shard_map/all_to_all | solution.py:193
  86.2 5.4 %all-to-all-done.3 = bf16[32,8,4]{1,2,0:T(4,128)(2,1)S(1)} async-done(((bf16[32,8,4]{1,2,0:T(4,128)(2,1)}), bf16[32,8,4]{1,2,0:T(4,128)(2,1)S(1)}, u32[]{:S(2)}, u32[]{:S(2)}) %all-to-all-start.3) | async-done | bytes 2080 | tf_op jit(solution)/shard_map/all_to_all | solution.py:193
  91.7 3.9 %all-to-all-start.4 = ((bf16[32,8,4,128]{3,2,1,0:T(4,128)(2,1)}), bf16[32,8,4,128]{3,2,1,0:T(4,128)(2,1)S(1)}, u32[]{:S(2)}, u32[]{:S(2)}) async-start(bf16[32,8,4,128]{3,2,1,0:T(4,128)(2,1)} %bitcast.29), calls=%async_computation.4 | async-start | bytes 524288 | tf_op jit(solution)/shard_map/all_to_all | solution.py:191
  95.5 7.2 %reshape.288 = bf16[256,4,2048]{2,1,0:T(4,128)(2,1)} reshape(bf16[2,512,2048]{2,1,0:T(8,128)(2,1)} %param.18) | data formatting | bytes 8388608 | tf_op jit(solution)/shard_map/reshape | solution.py:176
  102.7 12.1 %gather_fusion.4 = bf16[256,4,2048]{2,1,0:T(4,128)(2,1)} fusion(bf16[256,4,2048]{2,1,0:T(4,128)(2,1)} %reshape.288, s32[1024]{0:T(1024)S(1)} %pad_clamp_fusion), kind=kCustom, calls=%fused_computation.4 | custom fusion | bytes 8389632 | tf_op jit(solution)/shard_map/gather | solution.py:190
  114.9 7.9 %all-to-all-start.2 = ((bf16[32,8,4,2048]{3,2,1,0:T(4,128)(2,1)}), bf16[32,8,4,2048]{3,2,1,0:T(4,128)(2,1)}, u32[]{:S(2)}, u32[]{:S(2)}) async-start(bf16[32,8,4,2048]{3,2,1,0:T(4,128)(2,1)} %bitcast.88), calls=%async_computation.2 | async-start | bytes 8388608 | tf_op jit(solution)/shard_map/all_to_all | solution.py:190
  124.6 13.8 %collective-permute-start.2 = (bf16[128,1,512]{0,2,1:T(8,128)(2,1)}, bf16[128,1,512]{0,2,1:T(8,128)(2,1)}, u32[]{:S(2)}, u32[]{:S(2)}) collective-permute-start(bf16[128,1,512]{0,2,1:T(8,128)(2,1)} %get-tuple-element.142), channel_id=1, source_target_pairs={{0,1},{1,2},{2,3},{3,4},{4,5},{5,6},{6,7},{8,9},{9,10},{10,11},{11... | collective-permute-start | bytes 393224 | tf_op jit(solution)/shard_map/ppermute | solution.py:20
  142.3 4.3 %collective-permute-start.1 = (f32[128,2,1]{0,2,1:T(1,128)}, f32[128,2,1]{0,2,1:T(1,128)}, u32[]{:S(2)}, u32[]{:S(2)}) collective-permute-start(f32[128,2,1]{0,2,1:T(1,128)} %get-tuple-element.139), channel_id=1, source_target_pairs={{8,0},{16,8},{24,16},{32,24},{40,32},{48,40},{56,48},{64,56},{72,6... | collective-permute-start | bytes 3080 | tf_op jit(solution)/shard_map/ppermute | solution.py:22
  147.5 3.1 sort.17
  157.2 22.4 %all-to-all-done.2 = bf16[32,8,4,2048]{3,2,1,0:T(4,128)(2,1)} async-done(((bf16[32,8,4,2048]{3,2,1,0:T(4,128)(2,1)}), bf16[32,8,4,2048]{3,2,1,0:T(4,128)(2,1)}, u32[]{:S(2)}, u32[]{:S(2)}) %all-to-all-start.2) | async-done | bytes 4194336 | tf_op jit(solution)/shard_map/all_to_all | solution.py:190
  179.6 5.7 %gather_fusion.5 = bf16[128,4,2048]{2,1,0:T(4,128)(2,1)} fusion(bf16[256,4,2048]{2,1,0:T(4,128)(2,1)} %bitcast.25, s32[1024]{0:T(1024)S(1)} %pad_clamp_fusion.1), kind=kCustom, calls=%fused_computation.5 | custom fusion | bytes 4194816 | tf_op jit(solution)/shard_map/gather | solution.py:139
  185.4 2.5 reshape_reshape.16
  187.9 109.3 %while.21 = (s32[]{:T(128)}, f32[4,128,128]{2,1,0:T(8,128)}, f32[224]{0:T(256)S(1)}, bf16[4,128]{1,0:T(4,128)(2,1)}, bf16[4,128,2048]{2,1,0:T(8,128)(2,1)S(1)}, ...) while((s32[]{:T(128)}, f32[4,128,128]{2,1,0:T(8,128)}, ...), condition=%wide.region_6.7_spmd, body=%wide.region_3.6_spmd.sunk | while | flops 778973312 | bytes 50843112 | solution.py:88
  189.2 16.7 %exponential_multiply_fusion.2 = (f32[128,129,224]{0,2,1:T(8,128)}, f32[128,129,224]{0,2,1:T(8,128)S(1)}) fusion(f32[128]{0:T(128)S(1)} %get-tuple-element.229, f32[128,224]{0,1:T(8,128)S(1)} %broadcast_multiply_fusion.2, f32[128,128,16]{0,2,1:T(8,128)S(1)} %fusion.50, f32[16,224]{1,0:T(8,128)} %get-tuple-element.277), kind=kOutput, calls=%fused_computation.14.clone.2 | convolution fusion | flops 715739136 | bytes 30767616 | tf_op jit(solution)/shard_map/while/body/eval_jaxpr/cij,jg->cig/dot_general | solution.py:54
  206.8 6.8 %subtract_reduce_fusion.2 = f32[128,129]{0,1:T(8,128)S(1)} fusion(f32[128,129,224]{0,2,1:T(8,128)S(1)} %get-tuple-element.230, f32[128,224]{0,1:T(8,128)S(1)} %slice_bitcast_fusion.6, f32[128,224]{0,1:T(8,128)S(1)} %fusion.51, f32[128]{0:T(128)S(1)} %get-tuple-element.229, f32[128,224]{0,1:T(8,128)S(1)} %broadcast_multiply_fusion.2), kind=kLoop, calls=%fused_computation.13.clone.1 | loop fusion | flops 29572992 | bytes 15205376 | tf_op jit(solution)/shard_map/while/body/eval_jaxpr/reduce_sum | solution.py:66
  216.5 16.7 %exponential_multiply_fusion.2 = (f32[128,129,224]{0,2,1:T(8,128)}, f32[128,129,224]{0,2,1:T(8,128)S(1)}) fusion(f32[128]{0:T(128)S(1)} %get-tuple-element.229, f32[128,224]{0,1:T(8,128)S(1)} %broadcast_multiply_fusion.2, f32[128,128,16]{0,2,1:T(8,128)S(1)} %fusion.50, f32[16,224]{1,0:T(8,128)} %get-tuple-element.277), kind=kOutput, calls=%fused_computation.14.clone.2 | convolution fusion | flops 715739136 | bytes 30767616 | tf_op jit(solution)/shard_map/while/body/eval_jaxpr/cij,jg->cig/dot_general | solution.py:54
  234.2 6.8 %subtract_reduce_fusion.2 = f32[128,129]{0,1:T(8,128)S(1)} fusion(f32[128,129,224]{0,2,1:T(8,128)S(1)} %get-tuple-element.230, f32[128,224]{0,1:T(8,128)S(1)} %slice_bitcast_fusion.6, f32[128,224]{0,1:T(8,128)S(1)} %fusion.51, f32[128]{0:T(128)S(1)} %get-tuple-element.229, f32[128,224]{0,1:T(8,128)S(1)} %broadcast_multiply_fusion.2), kind=kLoop, calls=%fused_computation.13.clone.1 | loop fusion | flops 29572992 | bytes 15205376 | tf_op jit(solution)/shard_map/while/body/eval_jaxpr/reduce_sum | solution.py:66
  243.8 16.7 %exponential_multiply_fusion.2 = (f32[128,129,224]{0,2,1:T(8,128)}, f32[128,129,224]{0,2,1:T(8,128)S(1)}) fusion(f32[128]{0:T(128)S(1)} %get-tuple-element.229, f32[128,224]{0,1:T(8,128)S(1)} %broadcast_multiply_fusion.2, f32[128,128,16]{0,2,1:T(8,128)S(1)} %fusion.50, f32[16,224]{1,0:T(8,128)} %get-tuple-element.277), kind=kOutput, calls=%fused_computation.14.clone.2 | convolution fusion | flops 715739136 | bytes 30767616 | tf_op jit(solution)/shard_map/while/body/eval_jaxpr/cij,jg->cig/dot_general | solution.py:54
  261.5 6.8 %subtract_reduce_fusion.2 = f32[128,129]{0,1:T(8,128)S(1)} fusion(f32[128,129,224]{0,2,1:T(8,128)S(1)} %get-tuple-element.230, f32[128,224]{0,1:T(8,128)S(1)} %slice_bitcast_fusion.6, f32[128,224]{0,1:T(8,128)S(1)} %fusion.51, f32[128]{0:T(128)S(1)} %get-tuple-element.229, f32[128,224]{0,1:T(8,128)S(1)} %broadcast_multiply_fusion.2), kind=kLoop, calls=%fused_computation.13.clone.1 | loop fusion | flops 29572992 | bytes 15205376 | tf_op jit(solution)/shard_map/while/body/eval_jaxpr/reduce_sum | solution.py:66
  271.1 16.7 %exponential_multiply_fusion.2 = (f32[128,129,224]{0,2,1:T(8,128)}, f32[128,129,224]{0,2,1:T(8,128)S(1)}) fusion(f32[128]{0:T(128)S(1)} %get-tuple-element.229, f32[128,224]{0,1:T(8,128)S(1)} %broadcast_multiply_fusion.2, f32[128,128,16]{0,2,1:T(8,128)S(1)} %fusion.50, f32[16,224]{1,0:T(8,128)} %get-tuple-element.277), kind=kOutput, calls=%fused_computation.14.clone.2 | convolution fusion | flops 715739136 | bytes 30767616 | tf_op jit(solution)/shard_map/while/body/eval_jaxpr/cij,jg->cig/dot_general | solution.py:54
  288.8 6.8 %subtract_reduce_fusion.2 = f32[128,129]{0,1:T(8,128)S(1)} fusion(f32[128,129,224]{0,2,1:T(8,128)S(1)} %get-tuple-element.230, f32[128,224]{0,1:T(8,128)S(1)} %slice_bitcast_fusion.6, f32[128,224]{0,1:T(8,128)S(1)} %fusion.51, f32[128]{0:T(128)S(1)} %get-tuple-element.229, f32[128,224]{0,1:T(8,128)S(1)} %broadcast_multiply_fusion.2), kind=kLoop, calls=%fused_computation.13.clone.1 | loop fusion | flops 29572992 | bytes 15205376 | tf_op jit(solution)/shard_map/while/body/eval_jaxpr/reduce_sum | solution.py:66
  299.2 13.4 %scatter_fusion = f32[256,4,128]{2,1,0:T(4,128)} fusion(f32[256,4,128]{2,1,0:T(4,128)} %broadcast.233.clone, s32[128]{0:T(128)} %copy-done.9, f32[128,4,128]{2,1,0:T(4,128)S(1)} %broadcast_select_fusion.1), kind=kCustom, calls=%fused_computation.10 | custom fusion | bytes 786944 | tf_op jit(solution)/shard_map/scatter | solution.py:153
  312.7 3.9 %all-to-all-start.5 = ((f32[32,8,4,128]{3,2,1,0:T(4,128)}), f32[32,8,4,128]{3,2,1,0:T(4,128)S(1)}, u32[]{:S(2)}, u32[]{:S(2)}) async-start(f32[32,8,4,128]{3,2,1,0:T(4,128)} %bitcast.33), calls=%async_computation.5 | async-start | bytes 1048576 | tf_op jit(solution)/shard_map/all_to_all | solution.py:207
  320.7 11.9 %collective-permute-start.6 = (bf16[128,1,512]{0,2,1:T(8,128)(2,1)S(1)}, bf16[128,1,512]{0,2,1:T(8,128)(2,1)S(1)}, u32[]{:S(2)}, u32[]{:S(2)}) collective-permute-start(bf16[128,1,512]{0,2,1:T(8,128)(2,1)S(1)} %get-tuple-element.140), channel_id=1, source_target_pairs={{0,1},{1,2},{2,3},{3,4},{4,5},{5,6},{6,7},{8,9},{9,10},{10,11},{11... | collective-permute-start | bytes 393224 | tf_op jit(solution)/shard_map/ppermute | solution.py:20
  336.1 4.5 %collective-permute-start.5 = (f32[128,2,1]{0,2,1:T(1,128)S(1)}, f32[128,2,1]{0,2,1:T(1,128)S(1)}, u32[]{:S(2)}, u32[]{:S(2)}) collective-permute-start(f32[128,2,1]{0,2,1:T(1,128)S(1)} %get-tuple-element.137), channel_id=1, source_target_pairs={{8,0},{16,8},{24,16},{32,24},{40,32},{48,40},{56,48},{64,56},{72,6... | collective-permute-start | bytes 3080 | tf_op jit(solution)/shard_map/ppermute | solution.py:22
  340.6 2.2 collective-permute-done.7
  343.3 8.3 %scatter_fusion.1 = f32[256,4,128]{2,1,0:T(4,128)S(1)} fusion(f32[256,4,128]{2,1,0:T(4,128)S(1)} %broadcast.233, s32[256]{0:T(256)S(1)} %bitcast.99, f32[256,4,128]{2,1,0:T(4,128)S(1)} %bitcast.90), kind=kCustom, calls=%fused_computation.11 | custom fusion | flops 131072 | bytes 1573888 | tf_op jit(solution)/shard_map/scatter-add | solution.py:218
  (138 shorter events, 50.4 us)
Async XLA Ops:
  0.0 84.5 %copy-start = (bf16[2,512,128]{2,1,0:T(8,128)(2,1)S(1)}, bf16[2,512,128]{2,1,0:T(8,128)(2,1)}, u32[]{:S(2)}) copy-start(bf16[2,512,128]{2,1,0:T(8,128)(2,1)} %param.19) | copy-start | bytes 786436
  0.0 63.9 %copy-start.7 = (bf16[2,512]{1,0:T(2,128)(2,1)S(1)}, bf16[2,512]{1,0:T(2,128)(2,1)}, u32[]{:S(2)}) copy-start(bf16[2,512]{1,0:T(2,128)(2,1)} %param.20) | copy-start | bytes 6148
  0.0 73.6 %copy-start.8 = (bf16[2,512]{1,0:T(2,128)(2,1)S(1)}, bf16[2,512]{1,0:T(2,128)(2,1)}, u32[]{:S(2)}) copy-start(bf16[2,512]{1,0:T(2,128)(2,1)} %param.21) | copy-start | bytes 6148
  18.7 50.0 %all-to-all-start = ((bf16[32,1,8]{2,1,0:T(2,128)(2,1)}), bf16[32,1,8]{2,1,0:T(2,128)(2,1)S(1)}, u32[]{:S(2)}, u32[]{:S(2)}) async-start(bf16[32,1,8]{2,1,0:T(2,128)(2,1)} %copy.70), calls=%async_computation | async-start | bytes 32768 | tf_op jit(solution)/shard_map/all_to_all | solution.py:194
  63.7 59.1 %copy-start.3 = (f32[128,2,512]{2,1,0:T(2,128)S(1)}, f32[128,2,512]{2,1,0:T(2,128)}, u32[]{:S(2)}) copy-start(f32[128,2,512]{2,1,0:T(2,128)} %param.15) | copy-start | bytes 1572868
  64.9 82.4 %copy-start.5 = (f32[2,2,512]{2,1,0:T(2,128)S(1)}, f32[2,2,512]{2,1,0:T(2,128)}, u32[]{:S(2)}) copy-start(f32[2,2,512]{2,1,0:T(2,128)} %param.17) | copy-start | bytes 24580
  64.9 82.4 %copy-start.6 = (f32[2,2,512]{2,1,0:T(2,128)S(1)}, f32[2,2,512]{2,1,0:T(2,128)}, u32[]{:S(2)}) copy-start(f32[2,2,512]{2,1,0:T(2,128)} %param.16) | copy-start | bytes 24580
  68.6 12.1 %all-to-all-start.1 = ((bf16[32,8,4]{1,2,0:T(4,128)(2,1)}), bf16[32,8,4]{1,2,0:T(4,128)(2,1)S(1)}, u32[]{:S(2)}, u32[]{:S(2)}) async-start(bf16[32,8,4]{1,2,0:T(4,128)(2,1)} %copy.71), calls=%async_computation.1 | async-start | bytes 65536 | tf_op jit(solution)/shard_map/all_to_all | solution.py:192
  80.7 11.0 %all-to-all-start.3 = ((bf16[32,8,4]{1,2,0:T(4,128)(2,1)}), bf16[32,8,4]{1,2,0:T(4,128)(2,1)S(1)}, u32[]{:S(2)}, u32[]{:S(2)}) async-start(bf16[32,8,4]{1,2,0:T(4,128)(2,1)} %copy.73), calls=%async_computation.3 | async-start | bytes 65536 | tf_op jit(solution)/shard_map/all_to_all | solution.py:193
  91.7 23.2 %all-to-all-start.4 = ((bf16[32,8,4,128]{3,2,1,0:T(4,128)(2,1)}), bf16[32,8,4,128]{3,2,1,0:T(4,128)(2,1)S(1)}, u32[]{:S(2)}, u32[]{:S(2)}) async-start(bf16[32,8,4,128]{3,2,1,0:T(4,128)(2,1)} %bitcast.29), calls=%async_computation.4 | async-start | bytes 524288 | tf_op jit(solution)/shard_map/all_to_all | solution.py:191
  102.7 85.2 %copy-start.4 = (f32[224]{0:T(256)S(1)}, f32[224]{0:T(256)}, u32[]{:S(2)}) copy-start(f32[224]{0:T(256)} %param.23) | copy-start | bytes 2692
  114.9 64.7 %all-to-all-start.2 = ((bf16[32,8,4,2048]{3,2,1,0:T(4,128)(2,1)}), bf16[32,8,4,2048]{3,2,1,0:T(4,128)(2,1)}, u32[]{:S(2)}, u32[]{:S(2)}) async-start(bf16[32,8,4,2048]{3,2,1,0:T(4,128)(2,1)} %bitcast.88), calls=%async_computation.2 | async-start | bytes 8388608 | tf_op jit(solution)/shard_map/all_to_all | solution.py:190
  123.0 24.3 %copy-start.1 = (f32[128,2,512]{0,2,1:T(8,128)}, f32[128,2,512]{0,2,1:T(8,128)S(1)}, u32[]{:S(2)}) copy-start(f32[128,2,512]{0,2,1:T(8,128)S(1)} %copy.62) | copy-start | bytes 1572868
  123.0 0.8 copy-start.2
  124.6 192.8 %collective-permute-start.2 = (bf16[128,1,512]{0,2,1:T(8,128)(2,1)}, bf16[128,1,512]{0,2,1:T(8,128)(2,1)}, u32[]{:S(2)}, u32[]{:S(2)}) collective-permute-start(bf16[128,1,512]{0,2,1:T(8,128)(2,1)} %get-tuple-element.142), channel_id=1, source_target_pairs={{0,1},{1,2},{2,3},{3,4},{4,5},{5,6},{6,7},{8,9},{9,10},{10,11},{11... | collective-permute-start | bytes 393224 | tf_op jit(solution)/shard_map/ppermute | solution.py:20
  138.4 179.0 %collective-permute-start.3 = (bf16[128,1,512]{0,2,1:T(8,128)(2,1)}, bf16[128,1,512]{0,2,1:T(8,128)(2,1)}, u32[]{:S(2)}, u32[]{:S(2)}) collective-permute-start(bf16[128,1,512]{0,2,1:T(8,128)(2,1)} %get-tuple-element.143), channel_id=1, source_target_pairs={{1,0},{2,1},{3,2},{4,3},{5,4},{6,5},{7,6},{9,8},{10,9},{11,10},{12... | collective-permute-start | bytes 393224 | tf_op jit(solution)/shard_map/ppermute | solution.py:22
  140.9 177.6 %collective-permute-start = (f32[128,2,1]{0,2,1:T(1,128)}, f32[128,2,1]{0,2,1:T(1,128)}, u32[]{:S(2)}, u32[]{:S(2)}) collective-permute-start(f32[128,2,1]{0,2,1:T(1,128)} %get-tuple-element.138), channel_id=1, source_target_pairs={{0,8},{8,16},{16,24},{24,32},{32,40},{40,48},{48,56},{56,64},{64,7... | collective-permute-start | bytes 3080 | tf_op jit(solution)/shard_map/ppermute | solution.py:20
  142.3 176.2 %collective-permute-start.1 = (f32[128,2,1]{0,2,1:T(1,128)}, f32[128,2,1]{0,2,1:T(1,128)}, u32[]{:S(2)}, u32[]{:S(2)}) collective-permute-start(f32[128,2,1]{0,2,1:T(1,128)} %get-tuple-element.139), channel_id=1, source_target_pairs={{8,0},{16,8},{24,16},{32,24},{40,32},{48,40},{56,48},{64,56},{72,6... | collective-permute-start | bytes 3080 | tf_op jit(solution)/shard_map/ppermute | solution.py:22
  150.6 37.3 %copy-start.9 = (s32[128]{0:T(128)}, s32[128]{0:T(128)S(1)}, u32[]{:S(2)}) copy-start(s32[128]{0:T(128)S(1)} %compare_select_fusion.3) | copy-start | bytes 1540
  312.7 30.2 %all-to-all-start.5 = ((f32[32,8,4,128]{3,2,1,0:T(4,128)}), f32[32,8,4,128]{3,2,1,0:T(4,128)S(1)}, u32[]{:S(2)}, u32[]{:S(2)}) async-start(f32[32,8,4,128]{3,2,1,0:T(4,128)} %bitcast.33), calls=%async_computation.5 | async-start | bytes 1048576 | tf_op jit(solution)/shard_map/all_to_all | solution.py:207
  320.7 19.9 %collective-permute-start.6 = (bf16[128,1,512]{0,2,1:T(8,128)(2,1)S(1)}, bf16[128,1,512]{0,2,1:T(8,128)(2,1)S(1)}, u32[]{:S(2)}, u32[]{:S(2)}) collective-permute-start(bf16[128,1,512]{0,2,1:T(8,128)(2,1)S(1)} %get-tuple-element.140), channel_id=1, source_target_pairs={{0,1},{1,2},{2,3},{3,4},{4,5},{5,6},{6,7},{8,9},{9,10},{10,11},{11... | collective-permute-start | bytes 393224 | tf_op jit(solution)/shard_map/ppermute | solution.py:20
  332.6 10.1 %collective-permute-start.7 = (bf16[128,1,512]{0,2,1:T(8,128)(2,1)S(1)}, bf16[128,1,512]{0,2,1:T(8,128)(2,1)S(1)}, u32[]{:S(2)}, u32[]{:S(2)}) collective-permute-start(bf16[128,1,512]{0,2,1:T(8,128)(2,1)S(1)} %get-tuple-element.141), channel_id=1, source_target_pairs={{1,0},{2,1},{3,2},{4,3},{5,4},{6,5},{7,6},{9,8},{10,9},{11,10},{12... | collective-permute-start | bytes 393224 | tf_op jit(solution)/shard_map/ppermute | solution.py:22
  334.6 17.0 %collective-permute-start.4 = (f32[128,2,1]{0,2,1:T(1,128)S(1)}, f32[128,2,1]{0,2,1:T(1,128)S(1)}, u32[]{:S(2)}, u32[]{:S(2)}) collective-permute-start(f32[128,2,1]{0,2,1:T(1,128)S(1)} %get-tuple-element.136), channel_id=1, source_target_pairs={{0,8},{8,16},{16,24},{24,32},{32,40},{40,48},{48,56},{56,64},{64,7... | collective-permute-start | bytes 3080 | tf_op jit(solution)/shard_map/ppermute | solution.py:20
  336.1 15.5 %collective-permute-start.5 = (f32[128,2,1]{0,2,1:T(1,128)S(1)}, f32[128,2,1]{0,2,1:T(1,128)S(1)}, u32[]{:S(2)}, u32[]{:S(2)}) collective-permute-start(f32[128,2,1]{0,2,1:T(1,128)S(1)} %get-tuple-element.137), channel_id=1, source_target_pairs={{8,0},{16,8},{24,16},{32,24},{40,32},{48,40},{56,48},{64,56},{72,6... | collective-permute-start | bytes 3080 | tf_op jit(solution)/shard_map/ppermute | solution.py:22
where the time goes:
time: 355 us; the launch traced here: 353 us
  starting transfers between devices  109 us (31%)
  local copies, waits for them, and re-layouts  70.8 us (20%)
  matrix products  66.9 us (19%)
  other arithmetic  52.4 us (15%)
  waiting for transfers between devices  38.1 us (11%)
  blocking collectives  15.2 us (4%)
    dot_general x4, matrix products, column_heating(): jnp.einsum('cij,jg->cig', column_above, extinction_table, precision=lax.P...  66.9 us
    all_to_all x1, starting transfers between devices, per_device(): lax.all_to_all(active.astype(jnp.bfloat16), 'lon', split_axis=0, concat_a...  42.9 us
    ppermute x4, starting transfers between devices, padded(): lax.ppermute(tail, axis, [(i, (i + 1) % count) for i in range(ends)])  28.7 us
    reduce_sum x4, other arithmetic, column_heating(): net_flux = jnp.sum(downward - upward, axis=2)  27 us
    all_to_all x1, waiting for transfers between devices, per_device(): lax.all_to_all(block_abs[picked], 'lon', split_axis=0, concat_axis=0, til...  22.4 us
    unnamed x1, blocking collectives  15.2 us
    scatter x1, local copies, waits for them, and re-layouts, compute_filled(): jnp.zeros((slot_total, block_width, tier_number), jnp.float32).at[chosen]  13.4 us
    ppermute x4, starting transfers between devices, padded(): lax.ppermute(head, axis, [((i + 1) % count, i) for i in range(ends)])  12.7 us
  transfers between devices with their start and end apart: 14, of which 5 were waited for; matrix products, arithmetic and copies ran while one was open for 52% of the time, Pallas kernels for 0%

commit v1 on v0

v1 whole, which is shorter than its diff:
```python
import functools
import math

import jax
import jax.numpy as jnp
from jax import lax
from jax.experimental import pallas as pl
from jax.experimental.pallas import tpu as pltpu
from jax.sharding import PartitionSpec as P

DSTEPS = 2
DIFFUSE = 1.66
LOG2E = math.log2(math.e)
TIERS, TERMS, POINTS, BLOCK = 128, 16, 224, 4
RUN = 8
RUNS = TIERS // RUN
TILE = 256
ROWS = 8
LANES = 128


def across(row, rows):
    return jnp.broadcast_to(row, (rows, row.shape[1]))


def halves(values):
    high = values.astype(jnp.bfloat16)
    low = (values - high.astype(jnp.float32)).astype(jnp.bfloat16)
    return jnp.concatenate([high, low], axis=1)


def thirds(values):
    high = values.astype(jnp.bfloat16)
    left = values - high.astype(jnp.float32)
    middle = left.astype(jnp.bfloat16)
    low = (left - middle.astype(jnp.float32)).astype(jnp.bfloat16)
    return high, middle, low


def by_rows(left, right):
    return lax.dot_general(left, right, (((1,), (1,)), ((), ())), preferred_element_type=jnp.float32)


def rad_kernel(rows, tally_ref, gas_ref, mass_ref, cos_ref, alb_ref, order_ref, table_ref, light_ref, out_ref,
               lhs_ref, slope_ref, down_ref, up_ref, weight_ref, part_a, part_b, net_ref):
    width = 2 * TILE
    tiles = len(rows) * 2
    table = table_ref[...] * DIFFUSE
    table = jnp.concatenate([table, jnp.zeros((TERMS, 256 - POINTS), jnp.float32)], axis=1)
    stacked = jnp.concatenate([table] * RUN, axis=0).T[:POINTS]
    whole = halves(stacked * LOG2E)
    term = lax.broadcasted_iota(jnp.int32, (POINTS, 2 * LANES), 1) % LANES // TERMS
    for r in range(1, RUN + 1):
        chosen = jnp.where(term < r, whole.astype(jnp.float32), 0.0)
        lhs_ref[(r - 1) * POINTS:r * POINTS, :] = chosen.astype(jnp.bfloat16)
    light = jnp.concatenate([light_ref[...], jnp.ones((1, 256 - POINTS), jnp.float32)], axis=1)
    light = across(jnp.log(light) * LOG2E, LANES).T[:POINTS]
    light = jnp.concatenate([light, light], axis=1)
    eye = (lax.broadcasted_iota(jnp.int32, (LANES, LANES), 0)
           == lax.broadcasted_iota(jnp.int32, (LANES, LANES), 1)).astype(jnp.float32).astype(jnp.bfloat16)
    listed = across(order_ref[...].astype(jnp.float32), LANES).T
    rank = lax.broadcasted_iota(jnp.int32, listed.shape, 0)
    listed = jnp.where(rank < tally_ref[0, 0], listed, -1.0)

    for n in range(tiles):
        row, first = rows[n // 2], (n % 2) * TILE
        cols = slice(first, first + TILE)
        cosine = cos_ref[row:row + 1, cols].astype(jnp.float32)
        albedo = alb_ref[row:row + 1, cols].astype(jnp.float32)
        slope = -1.0 / (DIFFUSE * cosine)
        slope_ref[n] = across(slope, ROWS)
        amount = gas_ref[n // 2, cols, 0:LANES].astype(jnp.float32)
        for b in range(1, RUNS):
            amount = amount + gas_ref[n // 2, cols, b * LANES:(b + 1) * LANES].astype(jnp.float32)
        total = None
        for piece in thirds(amount):
            got = by_rows(whole, jnp.concatenate([piece, piece], axis=1))
            total = got if total is None else total + got
        floor = light + (jnp.log(albedo) * LOG2E) + (slope - 1.0) * total
        down_ref[n] = light
        up_ref[n] = floor
        top = jnp.exp2(light) - jnp.exp2(floor)
        net_ref[n] = jnp.sum(top.reshape(POINTS // ROWS, ROWS, TILE), axis=0)
        mass = by_rows(eye, mass_ref[n // 2, cols, :])
        lit = []
        for t in range(TILE // LANES):
            block = (lax.broadcasted_iota(jnp.int32, listed.shape, 1) + (row * width + first + t * LANES)) // BLOCK
            hit = jnp.where(listed == block.astype(jnp.float32), 1.0, 0.0)
            lit.append(jnp.sum(hit, axis=0, keepdims=True))
        lit = jnp.concatenate(lit, axis=1)
        weight_ref[n] = cosine * lit / mass

    def parts(n):
        tile, b = n // RUNS, n % RUNS
        g = gas_ref[tile // 2, pl.ds(pl.multiple_of(tile % 2 * TILE, TILE), TILE),
                    pl.ds(pl.multiple_of(b * LANES, LANES), LANES)]
        return by_rows(lhs_ref[...], jnp.concatenate([g, g], axis=1))

    def process(part_ref, n):
        tile, b = n // RUNS, n % RUNS
        levels = pl.ds(pl.multiple_of(b * RUN, RUN), RUN)
        for t in range(TILE // LANES):
            cols = slice(t * LANES, (t + 1) * LANES)
            s = slope_ref[tile, :, cols]
            acc = [None] * (RUN + 1)
            for q in range(POINTS // ROWS):
                here = slice(q * ROWS, (q + 1) * ROWS)
                down0 = down_ref[tile, here, cols]
                up0 = up_ref[tile, here, cols]
                for r in range(1, RUN + 1):
                    at = (r - 1) * POINTS + q * ROWS
                    part = part_ref[at:at + ROWS, cols]
                    down = s * part + down0
                    up = part + up0
                    value = jnp.exp2(down) - jnp.exp2(up)
                    acc[r] = value if acc[r] is None else acc[r] + value
                down_ref[tile, here, cols] = down
                up_ref[tile, here, cols] = up
            acc[0] = net_ref[tile, :, cols]
            net_ref[tile, :, cols] = acc[RUN]
            diffs = []
            for r in range(1, RUN + 1):
                diffs.append(jnp.sum(acc[r - 1] - acc[r], axis=0, keepdims=True))
            place = pl.ds(pl.multiple_of(tile % 2 * TILE + t * LANES, LANES), LANES)
            out_ref[tile // 2, levels, place] = jnp.concatenate(diffs, axis=0) * weight_ref[tile, levels, cols]

    part_a[...] = parts(0)
    last = tiles * RUNS - 1

    def two_runs(h, carry):
        n = 2 * h
        part_b[...] = parts(n + 1)
        process(part_a, n)
        part_a[...] = parts(jnp.minimum(n + 2, last))
        process(part_b, n + 1)
        return carry

    lax.fori_loop(0, tiles * RUNS // 2, two_runs, 0)


def radiation(gas, mass, cosine, albedo, order, table, light, tally, rows=(0, 1)):
    tiles = 2 * len(rows)
    whole = lambda shape: pl.BlockSpec(shape, lambda: (0,) * len(shape))
    n = len(rows)
    return pl.pallas_call(
        functools.partial(rad_kernel, rows),
        out_shape=jax.ShapeDtypeStruct((n, TIERS, 512), jnp.float32),
        in_specs=[
            pl.BlockSpec(memory_space=pltpu.SMEM),
            pl.BlockSpec((n, 512, TIERS * TERMS), lambda: (rows[0] // n, 0, 0)),
            pl.BlockSpec((n, 512, TIERS), lambda: (rows[0] // n, 0, 0)),
            whole((2, 512)), whole((2, 512)), whole((1, 256)), whole((TERMS, POINTS)), whole((1, POINTS)),
        ],
        out_specs=whole((n, TIERS, 512)),
        scratch_shapes=[
            pltpu.VMEM((RUN * POINTS, 2 * LANES), jnp.bfloat16),
            pltpu.VMEM((tiles, ROWS, TILE), jnp.float32),
            pltpu.VMEM((tiles, POINTS, TILE), jnp.float32),
            pltpu.VMEM((tiles, POINTS, TILE), jnp.float32),
            pltpu.VMEM((tiles, TIERS, TILE), jnp.float32),
            pltpu.VMEM((RUN * POINTS, TILE), jnp.float32),
            pltpu.VMEM((RUN * POINTS, TILE), jnp.float32),
            pltpu.VMEM((tiles, ROWS, TILE), jnp.float32),
        ],
        compiler_params=pltpu.CompilerParams(vmem_limit_bytes=40 * 1024 * 1024),
    )(tally, gas, mass, cosine, albedo, order, table, light)

def padded(cells, sides, width, closed):
    for axis, dim in sides:
        count = lax.axis_size(axis)
        ends = count if closed else count - 1
        head = lax.slice_in_dim(cells, 0, width, axis=dim)
        tail = lax.slice_in_dim(cells, cells.shape[dim] - width, cells.shape[dim], axis=dim)
        cells = jnp.concatenate(
            [
                lax.ppermute(tail, axis, [(i, (i + 1) % count) for i in range(ends)]),
                cells,
                lax.ppermute(head, axis, [((i + 1) % count, i) for i in range(ends)]),
            ],
            axis=dim,
        )
    return cells


def march_forward(thermal_field, zonal_weights, meridional_weights):
    prognostic_field = thermal_field
    for step_index in range(DSTEPS):
        lon_rims = padded(prognostic_field, (("lon", 2),), 1, True)
        lat_rims = padded(prognostic_field.astype(jnp.bfloat16), (("lat", 1),), 1, False).astype(
            prognostic_field.dtype
        )
        western = lon_rims[:, :, :-2]
        eastern = lon_rims[:, :, 2:]
        southern = lat_rims[:, :-2, :]
        northern = lat_rims[:, 2:, :]
        prognostic_field = (
            prognostic_field
            + zonal_weights[0] * (western - prognostic_field)
            + zonal_weights[1] * (eastern - prognostic_field)
            + meridional_weights[0] * (southern - prognostic_field)
            + meridional_weights[1] * (northern - prognostic_field)
        )
    return prognostic_field


def per_device(
    thermal_field,
    zonal_weights,
    meridional_weights,
    gas_burden,
    tier_air_weight,
    solar_elevation_factor,
    ground_reflectance,
    extinction_table,
    incoming_irradiance,
    daytime_tile_tally,
    daytime_tile_order,
):
    prognostic_field = march_forward(thermal_field, zonal_weights, meridional_weights)
    heat = radiation(
        gas_burden,
        tier_air_weight,
        solar_elevation_factor,
        ground_reflectance,
        daytime_tile_order.reshape(1, -1),
        extinction_table,
        incoming_irradiance.reshape(1, -1),
        daytime_tile_tally,
    )
    return prognostic_field + heat.transpose(1, 0, 2)


def solution(mesh):
    placed = (
        P(None, "lat", "lon"),
        P(None, "lat", "lon"),
        P(None, "lat", "lon"),
        P("lat", "lon", None),
        P("lat", "lon", None),
        P("lat", "lon"),
        P("lat", "lon"),
        P(),
        P(),
        P("lat", "lon"),
        P("lat", "lon", None),
    )
    return jax.shard_map(
        per_device, mesh=mesh, in_specs=placed, out_specs=P(None, "lat", "lon"), check_vma=False
    )
```

time: 355 us -> 88.2 us (0.25)
  starting transfers between devices: 109 us -> 28.3 us
  matrix products: 66.9 us -> 0 us
  local copies, waits for them, and re-layouts: 70.8 us -> 10.3 us
  other arithmetic: 52.4 us -> 1.17 us
  Pallas kernels: 0 us -> 42.4 us
  waiting for transfers between devices: 38.1 us -> 4.69 us
  blocking collectives: 15.2 us -> 0 us
    all_to_all x6 -> x0, starting transfers between devices: 67.3 us -> none  [the longest x1 42.9 us: per_device(): lax.all_to_all(active.astype(jnp.bfloat16), 'lon', split_axis=0, concat_a...]
    dot_general x4 -> x0, matrix products: 66.9 us -> none  [column_heating(): jnp.einsum('cij,jg->cig', column_above, extinction_table, precision=lax.P...]
    pallas_call x0 -> x1, Pallas kernels: none -> 42.4 us  [radiation(): pl.pallas_call(functools.partial(rad_kernel, rows), out_shape=jax.ShapeDt...]
    all_to_all x6 -> x0, waiting for transfers between devices: 35.9 us -> none  [the longest x1 22.4 us: per_device(): lax.all_to_all(block_abs[picked], 'lon', split_axis=0, concat_axis=0, til...]
    gather x13 -> x0, local copies, waits for them, and re-layouts: 29.7 us -> none  [the longest x1 12.1 us: per_device(): block_abs[picked]]
    reduce_sum x4 -> x0, other arithmetic: 27 us -> none  [column_heating(): net_flux = jnp.sum(downward - upward, axis=2)]
    unnamed x1 -> x0, blocking collectives: 15.2 us -> none
    ppermute x4, starting transfers between devices: 28.7 us -> 13.9 us  [padded(): lax.ppermute(tail, axis, [(i, (i + 1) % count) for i in range(ends)])]
  transfers between devices with their start and end apart: 14 -> 8, of which waited for: 5 -> 2; matrix products, arithmetic and copies ran while one was open for 52% -> 2% of each run, Pallas kernels for 0% -> 48%
where the time goes in v1:
time: 88.2 us; the launch traced here: 87.7 us
  Pallas kernels  42.4 us (48%)
  starting transfers between devices  28.3 us (32%)
  local copies, waits for them, and re-layouts  10.3 us (12%)
  waiting for transfers between devices  4.69 us (5%)
  other arithmetic  1.17 us (1%)
    pallas_call x1, Pallas kernels, radiation(): pl.pallas_call(functools.partial(rad_kernel, rows), out_shape=jax.ShapeDt...  42.4 us
    ppermute x4, starting transfers between devices, padded(): lax.ppermute(head, axis, [((i + 1) % count, i) for i in range(ends)])  14.5 us
    ppermute x4, starting transfers between devices, padded(): lax.ppermute(tail, axis, [(i, (i + 1) % count) for i in range(ends)])  13.9 us
    unnamed x20, local copies, waits for them, and re-layouts  8.87 us
    ppermute x4, waiting for transfers between devices, padded(): lax.ppermute(tail, axis, [(i, (i + 1) % count) for i in range(ends)])  3.83 us
  transfers between devices with their start and end apart: 8, of which 2 were waited for; matrix products, arithmetic and copies ran while one was open for 2% of the time, Pallas kernels for 48%

profile of v1, /device:TPU:65, one launch (start us, length us, event | category | flops | bytes accessed | tf_op | source)
XLA Modules:
  0.0 87.7 jit_solution(8949535372767399532)
XLA Ops:
  0.0 1.1 %copy.24 = bf16[128,2,512]{2,0,1:T(8,128)(2,1)S(1)} copy(f32[128,2,512]{2,1,0:T(2,128)} %param.11) | data formatting | bytes 786432 | tf_op args[0]
  1.2 6.7 %collective-permute-start.2 = (bf16[128,1,512]{2,0,1:T(8,128)(2,1)S(1)}, bf16[128,1,512]{2,0,1:T(8,128)(2,1)S(1)}, u32[]{:S(2)}, u32[]{:S(2)}) collective-permute-start(bf16[128,1,512]{2,0,1:T(8,128)(2,1)S(1)} %get-tuple-element.13), channel_id=1, source_target_pairs={{0,1},{1,2},{2,3},{3,4},{4,5},{5,6},{6,7},{8,9},{9,10},{10,11},{11... | collective-permute-start | bytes 393224 | tf_op jit(solution)/shard_map/ppermute | solution.py:176
  7.9 1.9 %collective-permute-start.3 = (bf16[128,1,512]{2,0,1:T(8,128)(2,1)S(1)}, bf16[128,1,512]{2,0,1:T(8,128)(2,1)S(1)}, u32[]{:S(2)}, u32[]{:S(2)}) collective-permute-start(bf16[128,1,512]{2,0,1:T(8,128)(2,1)S(1)} %get-tuple-element.14), channel_id=1, source_target_pairs={{1,0},{2,1},{3,2},{4,3},{5,4},{6,5},{7,6},{9,8},{10,9},{11,10},{12... | collective-permute-start | bytes 393224 | tf_op jit(solution)/shard_map/ppermute | solution.py:178
  9.8 1.1 %copy.15 = f32[128,2,512]{2,0,1:T(8,128)S(1)} copy(f32[128,2,512]{2,1,0:T(2,128)} %param.11) | data formatting | bytes 1048576 | tf_op args[0]
  10.9 0.1 fusion.24
  11.0 0.8 collective-permute-start
  11.9 4.9 %collective-permute-start.1 = (f32[128,2,1]{2,0,1:T(8,128)S(1)}, f32[128,2,1]{2,0,1:T(8,128)S(1)}, u32[]{:S(2)}, u32[]{:S(2)}) collective-permute-start(f32[128,2,1]{2,0,1:T(8,128)S(1)} %get-tuple-element.10), channel_id=1, source_target_pairs={{8,0},{16,8},{24,16},{32,24},{40,32},{48,40},{56,48},{64,56},{72,6... | collective-permute-start | bytes 3080 | tf_op jit(solution)/shard_map/ppermute | solution.py:178
  17.5 0.0 copy-start
  17.5 2.2 %copy-done = bf16[2,512,2048]{2,1,0:T(8,128)(2,1)S(1)} copy-done((bf16[2,512,2048]{2,1,0:T(8,128)(2,1)S(1)}, bf16[2,512,2048]{2,1,0:T(8,128)(2,1)}, u32[]{:S(2)}) %copy-start) | copy-done | bytes 4194328
  19.6 0.9 %copy-done.1 = bf16[2,512,128]{2,1,0:T(8,128)(2,1)S(1)} copy-done((bf16[2,512,128]{2,1,0:T(8,128)(2,1)S(1)}, bf16[2,512,128]{2,1,0:T(8,128)(2,1)}, u32[]{:S(2)}) %copy-start.1) | copy-done | bytes 262168
  20.6 0.7 copy-done.2
  21.3 0.7 copy-done.3
  22.0 0.7 copy-done.4
  22.7 0.7 copy-done.5
  23.4 0.7 copy-done.6
  24.0 42.4 %shard_map.109 = f32[2,128,512]{2,1,0:T(8,128)S(1)} custom-call(s32[1,1]{1,0:T(1,128)S(6)} %copy.25.tally_ref, bf16[2,512,2048]{2,1,0:T(8,128)(2,1)S(1)} %copy-done, bf16[2,512,128]{2,1,0:T(8,128)(2,1)S(1)} %copy-done.1, bf16[2,512]{1,0:T(2,128)(2,1)S(1)} %copy-done.3, bf16[2,512]{1,0:T(2,128)(2,1)S(1)} %copy-done.4, s32[1,256]{1,0:T(1,128)S(1)} %bitcast.12, ...), custom_call_target="tpu_custom_call" | custom-call | tf_op jit(solution)/shard_map/pallas_call | solution.py:145
  66.5 0.0 collective-permute-done.2
  66.5 0.0 collective-permute-done.3
  66.5 0.1 maximum_convert_fusion
  66.6 0.0 collective-permute-done
  66.6 0.0 collective-permute-done.1
  66.6 0.5 fusion.21
  67.1 6.3 %collective-permute-start.6 = (bf16[128,1,512]{2,0,1:T(8,128)(2,1)S(1)}, bf16[128,1,512]{2,0,1:T(8,128)(2,1)S(1)}, u32[]{:S(2)}, u32[]{:S(2)}) collective-permute-start(bf16[128,1,512]{2,0,1:T(8,128)(2,1)S(1)} %get-tuple-element.11), channel_id=1, source_target_pairs={{0,1},{1,2},{2,3},{3,4},{4,5},{5,6},{6,7},{8,9},{9,10},{10,11},{11... | collective-permute-start | bytes 393224 | tf_op jit(solution)/shard_map/ppermute | solution.py:176
  73.5 1.9 %collective-permute-start.7 = (bf16[128,1,512]{2,0,1:T(8,128)(2,1)S(1)}, bf16[128,1,512]{2,0,1:T(8,128)(2,1)S(1)}, u32[]{:S(2)}, u32[]{:S(2)}) collective-permute-start(bf16[128,1,512]{2,0,1:T(8,128)(2,1)S(1)} %get-tuple-element.12), channel_id=1, source_target_pairs={{1,0},{2,1},{3,2},{4,3},{5,4},{6,5},{7,6},{9,8},{10,9},{11,10},{12... | collective-permute-start | bytes 393224 | tf_op jit(solution)/shard_map/ppermute | solution.py:178
  75.4 0.1 fusion.23
  75.5 0.1 collective-permute-start.4
  75.6 5.7 %collective-permute-start.5 = (f32[128,2,1]{2,0,1:T(8,128)S(1)}, f32[128,2,1]{2,0,1:T(8,128)S(1)}, u32[]{:S(2)}, u32[]{:S(2)}) collective-permute-start(f32[128,2,1]{2,0,1:T(8,128)S(1)} %get-tuple-element.8), channel_id=1, source_target_pairs={{8,0},{16,8},{24,16},{32,24},{40,32},{48,40},{56,48},{64,56},{72,6... | collective-permute-start | bytes 3080 | tf_op jit(solution)/shard_map/ppermute | solution.py:178
  81.2 0.9 collective-permute-done.7
  82.1 0.1 maximum_convert_fusion.1
  82.2 3.8 %collective-permute-done.4 = f32[128,2,1]{2,0,1:T(8,128)S(1)} collective-permute-done((f32[128,2,1]{2,0,1:T(8,128)S(1)}, f32[128,2,1]{2,0,1:T(8,128)S(1)}, u32[]{:S(2)}, u32[]{:S(2)}) %collective-permute-start.4) | collective-permute-done | bytes 1056 | tf_op jit(solution)/shard_map/ppermute | solution.py:176
  86.0 0.5 fusion.2
  86.5 1.2 %copy.22 = f32[128,2,512]{2,1,0:T(2,128)} copy(f32[128,2,512]{2,0,1:T(8,128)S(1)} %fusion.2) | data formatting | bytes 1048576 | tf_op jit(solution)/shard_map/add | solution.py:230
  (15 shorter events, 0.1 us)
Async XLA Ops:
  0.0 66.5 %copy-start.8 = (f32[2,2,512]{2,1,0:T(2,128)S(1)}, f32[2,2,512]{2,1,0:T(2,128)}, u32[]{:S(2)}) copy-start(f32[2,2,512]{2,1,0:T(2,128)} %param.12) | copy-start | bytes 24580
  0.0 66.5 %copy-start.7 = (f32[2,2,512]{2,1,0:T(2,128)S(1)}, f32[2,2,512]{2,1,0:T(2,128)}, u32[]{:S(2)}) copy-start(f32[2,2,512]{2,1,0:T(2,128)} %param.13) | copy-start | bytes 24580
  1.2 65.3 %collective-permute-start.2 = (bf16[128,1,512]{2,0,1:T(8,128)(2,1)S(1)}, bf16[128,1,512]{2,0,1:T(8,128)(2,1)S(1)}, u32[]{:S(2)}, u32[]{:S(2)}) collective-permute-start(bf16[128,1,512]{2,0,1:T(8,128)(2,1)S(1)} %get-tuple-element.13), channel_id=1, source_target_pairs={{0,1},{1,2},{2,3},{3,4},{4,5},{5,6},{6,7},{8,9},{9,10},{10,11},{11... | collective-permute-start | bytes 393224 | tf_op jit(solution)/shard_map/ppermute | solution.py:176
  7.9 58.6 %collective-permute-start.3 = (bf16[128,1,512]{2,0,1:T(8,128)(2,1)S(1)}, bf16[128,1,512]{2,0,1:T(8,128)(2,1)S(1)}, u32[]{:S(2)}, u32[]{:S(2)}) collective-permute-start(bf16[128,1,512]{2,0,1:T(8,128)(2,1)S(1)} %get-tuple-element.14), channel_id=1, source_target_pairs={{1,0},{2,1},{3,2},{4,3},{5,4},{6,5},{7,6},{9,8},{10,9},{11,10},{12... | collective-permute-start | bytes 393224 | tf_op jit(solution)/shard_map/ppermute | solution.py:178
  11.0 55.6 %collective-permute-start = (f32[128,2,1]{2,0,1:T(8,128)S(1)}, f32[128,2,1]{2,0,1:T(8,128)S(1)}, u32[]{:S(2)}, u32[]{:S(2)}) collective-permute-start(f32[128,2,1]{2,0,1:T(8,128)S(1)} %get-tuple-element.9), channel_id=1, source_target_pairs={{0,8},{8,16},{16,24},{24,32},{32,40},{40,48},{48,56},{56,64},{64,7... | collective-permute-start | bytes 3080 | tf_op jit(solution)/shard_map/ppermute | solution.py:176
  11.9 54.8 %collective-permute-start.1 = (f32[128,2,1]{2,0,1:T(8,128)S(1)}, f32[128,2,1]{2,0,1:T(8,128)S(1)}, u32[]{:S(2)}, u32[]{:S(2)}) collective-permute-start(f32[128,2,1]{2,0,1:T(8,128)S(1)} %get-tuple-element.10), channel_id=1, source_target_pairs={{8,0},{16,8},{24,16},{32,24},{40,32},{48,40},{56,48},{64,56},{72,6... | collective-permute-start | bytes 3080 | tf_op jit(solution)/shard_map/ppermute | solution.py:178
  17.5 2.2 %copy-start = (bf16[2,512,2048]{2,1,0:T(8,128)(2,1)S(1)}, bf16[2,512,2048]{2,1,0:T(8,128)(2,1)}, u32[]{:S(2)}) copy-start(bf16[2,512,2048]{2,1,0:T(8,128)(2,1)} %gas_ref.1) | copy-start | bytes 12582916
  19.6 0.9 %copy-start.1 = (bf16[2,512,128]{2,1,0:T(8,128)(2,1)S(1)}, bf16[2,512,128]{2,1,0:T(8,128)(2,1)}, u32[]{:S(2)}) copy-start(bf16[2,512,128]{2,1,0:T(8,128)(2,1)} %mass_ref.1) | copy-start | bytes 786436
  20.6 0.7 copy-start.2
  21.3 0.7 copy-start.3
  22.0 0.7 copy-start.4
  22.7 0.7 copy-start.5
  23.4 0.7 copy-start.6
  67.1 14.1 %collective-permute-start.6 = (bf16[128,1,512]{2,0,1:T(8,128)(2,1)S(1)}, bf16[128,1,512]{2,0,1:T(8,128)(2,1)S(1)}, u32[]{:S(2)}, u32[]{:S(2)}) collective-permute-start(bf16[128,1,512]{2,0,1:T(8,128)(2,1)S(1)} %get-tuple-element.11), channel_id=1, source_target_pairs={{0,1},{1,2},{2,3},{3,4},{4,5},{5,6},{6,7},{8,9},{9,10},{10,11},{11... | collective-permute-start | bytes 393224 | tf_op jit(solution)/shard_map/ppermute | solution.py:176
  73.5 8.7 %collective-permute-start.7 = (bf16[128,1,512]{2,0,1:T(8,128)(2,1)S(1)}, bf16[128,1,512]{2,0,1:T(8,128)(2,1)S(1)}, u32[]{:S(2)}, u32[]{:S(2)}) collective-permute-start(bf16[128,1,512]{2,0,1:T(8,128)(2,1)S(1)} %get-tuple-element.12), channel_id=1, source_target_pairs={{1,0},{2,1},{3,2},{4,3},{5,4},{6,5},{7,6},{9,8},{10,9},{11,10},{12... | collective-permute-start | bytes 393224 | tf_op jit(solution)/shard_map/ppermute | solution.py:178
  75.5 10.5 %collective-permute-start.4 = (f32[128,2,1]{2,0,1:T(8,128)S(1)}, f32[128,2,1]{2,0,1:T(8,128)S(1)}, u32[]{:S(2)}, u32[]{:S(2)}) collective-permute-start(f32[128,2,1]{2,0,1:T(8,128)S(1)} %get-tuple-element.7), channel_id=1, source_target_pairs={{0,8},{8,16},{16,24},{24,32},{32,40},{40,48},{48,56},{56,64},{64,7... | collective-permute-start | bytes 3080 | tf_op jit(solution)/shard_map/ppermute | solution.py:176
  75.6 10.4 %collective-permute-start.5 = (f32[128,2,1]{2,0,1:T(8,128)S(1)}, f32[128,2,1]{2,0,1:T(8,128)S(1)}, u32[]{:S(2)}, u32[]{:S(2)}) collective-permute-start(f32[128,2,1]{2,0,1:T(8,128)S(1)} %get-tuple-element.8), channel_id=1, source_target_pairs={{8,0},{16,8},{24,16},{32,24},{40,32},{48,40},{56,48},{64,56},{72,6... | collective-permute-start | bytes 3080 | tf_op jit(solution)/shard_map/ppermute | solution.py:178

commit v2 on v1

--- a/solution.py
+++ b/solution.py
@@ -17,6 +17,9 @@
 TILE = 256
 ROWS = 8
 LANES = 128
+TOGETHER = 4
+HALO = 128
+VMEM_BYTES = 60 * 1024 * 1024
 
 
 def across(row, rows):
@@ -41,10 +44,20 @@
     return lax.dot_general(left, right, (((1,), (1,)), ((), ())), preferred_element_type=jnp.float32)
 
 
-def rad_kernel(rows, tally_ref, gas_ref, mass_ref, cos_ref, alb_ref, order_ref, table_ref, light_ref, out_ref,
-               lhs_ref, slope_ref, down_ref, up_ref, weight_ref, part_a, part_b, net_ref):
+def rad_kernel(rows, tally_ref, gas_hbm, mass_hbm, cos_ref, alb_ref, order_ref, table_ref, light_ref, out_ref,
+               lhs_ref, slope_ref, down_ref, up_ref, weight_ref, part_a, part_b, net_ref,
+               gas_ref, mass_ref, gas_sem, mass_sem):
     width = 2 * TILE
     tiles = len(rows) * 2
+    gas_copies, mass_copies = [], []
+    for n in range(tiles):
+        cols = slice(n % 2 * TILE, (n % 2 + 1) * TILE)
+        gas_copies.append(pltpu.make_async_copy(
+            gas_hbm.at[rows[n // 2], cols], gas_ref.at[n // 2, cols], gas_sem.at[n]))
+        mass_copies.append(pltpu.make_async_copy(
+            mass_hbm.at[rows[n // 2], cols], mass_ref.at[n // 2, cols], mass_sem.at[n]))
+    for copy in gas_copies + mass_copies:
+        copy.start()
     table = table_ref[...] * DIFFUSE
     table = jnp.concatenate([table, jnp.zeros((TERMS, 256 - POINTS), jnp.float32)], axis=1)
     stacked = jnp.concatenate([table] * RUN, axis=0).T[:POINTS]
@@ -69,6 +82,8 @@
         albedo = alb_ref[row:row + 1, cols].astype(jnp.float32)
         slope = -1.0 / (DIFFUSE * cosine)
         slope_ref[n] = across(slope, ROWS)
+        gas_copies[n].wait()
+        mass_copies[n].wait()
         amount = gas_ref[n // 2, cols, 0:LANES].astype(jnp.float32)
         for b in range(1, RUNS):
             amount = amount + gas_ref[n // 2, cols, b * LANES:(b + 1) * LANES].astype(jnp.float32)
@@ -91,13 +106,13 @@
         weight_ref[n] = cosine * lit / mass
 
     def parts(n):
-        tile, b = n // RUNS, n % RUNS
-        g = gas_ref[tile // 2, pl.ds(pl.multiple_of(tile % 2 * TILE, TILE), TILE),
+        tile, b = n >> 4, n & (RUNS - 1)
+        g = gas_ref[tile >> 1, pl.ds(pl.multiple_of((tile & 1) * TILE, TILE), TILE),
                     pl.ds(pl.multiple_of(b * LANES, LANES), LANES)]
         return by_rows(lhs_ref[...], jnp.concatenate([g, g], axis=1))
 
     def process(part_ref, n):
-        tile, b = n // RUNS, n % RUNS
+        tile, b = n >> 4, n & (RUNS - 1)
         levels = pl.ds(pl.multiple_of(b * RUN, RUN), RUN)
         for t in range(TILE // LANES):
             cols = slice(t * LANES, (t + 1) * LANES)
@@ -112,8 +127,8 @@
                     part = part_ref[at:at + ROWS, cols]
                     down = s * part + down0
                     up = part + up0
-                    value = jnp.exp2(down) - jnp.exp2(up)
-                    acc[r] = value if acc[r] is None else acc[r] + value
+                    light = jnp.exp2(down)
+                    acc[r] = (light if acc[r] is None else acc[r] + light) - jnp.exp2(up)
                 down_ref[tile, here, cols] = down
                 up_ref[tile, here, cols] = up
             acc[0] = net_ref[tile, :, cols]
@@ -121,21 +136,21 @@
             diffs = []
             for r in range(1, RUN + 1):
                 diffs.append(jnp.sum(acc[r - 1] - acc[r], axis=0, keepdims=True))
-            place = pl.ds(pl.multiple_of(tile % 2 * TILE + t * LANES, LANES), LANES)
-            out_ref[tile // 2, levels, place] = jnp.concatenate(diffs, axis=0) * weight_ref[tile, levels, cols]
+            place = pl.ds(pl.multiple_of((tile & 1) * TILE + t * LANES, LANES), LANES)
+            out_ref[tile >> 1, levels, place] = jnp.concatenate(diffs, axis=0) * weight_ref[tile, levels, cols]
 
     part_a[...] = parts(0)
     last = tiles * RUNS - 1
 
-    def two_runs(h, carry):
-        n = 2 * h
-        part_b[...] = parts(n + 1)
-        process(part_a, n)
-        part_a[...] = parts(jnp.minimum(n + 2, last))
-        process(part_b, n + 1)
+    def some_runs(h, carry):
+        for u in range(TOGETHER):
+            n = TOGETHER * h + u
+            now, later = (part_a, part_b) if u % 2 == 0 else (part_b, part_a)
+            later[...] = parts(jnp.minimum(n + 1, last))
+            process(now, n)
         return carry
 
-    lax.fori_loop(0, tiles * RUNS // 2, two_runs, 0)
+    lax.fori_loop(0, tiles * RUNS // TOGETHER, some_runs, 0)
 
 
 def radiation(gas, mass, cosine, albedo, order, table, light, tally, rows=(0, 1)):
@@ -147,8 +162,8 @@
         out_shape=jax.ShapeDtypeStruct((n, TIERS, 512), jnp.float32),
         in_specs=[
             pl.BlockSpec(memory_space=pltpu.SMEM),
-            pl.BlockSpec((n, 512, TIERS * TERMS), lambda: (rows[0] // n, 0, 0)),
-            pl.BlockSpec((n, 512, TIERS), lambda: (rows[0] // n, 0, 0)),
+            pl.BlockSpec(memory_space=pl.ANY),
+            pl.BlockSpec(memory_space=pl.ANY),
             whole((2, 512)), whole((2, 512)), whole((1, 256)), whole((TERMS, POINTS)), whole((1, POINTS)),
         ],
         out_specs=whole((n, TIERS, 512)),
@@ -161,46 +176,95 @@
             pltpu.VMEM((RUN * POINTS, TILE), jnp.float32),
             pltpu.VMEM((RUN * POINTS, TILE), jnp.float32),
             pltpu.VMEM((tiles, ROWS, TILE), jnp.float32),
+            pltpu.VMEM((n, 512, TIERS * TERMS), jnp.bfloat16),
+            pltpu.VMEM((n, 512, TIERS), jnp.bfloat16),
+            pltpu.SemaphoreType.DMA((tiles,)),
+            pltpu.SemaphoreType.DMA((tiles,)),
         ],
-        compiler_params=pltpu.CompilerParams(vmem_limit_bytes=40 * 1024 * 1024),
+        compiler_params=pltpu.CompilerParams(vmem_limit_bytes=VMEM_BYTES),
+        cost_estimate=pl.CostEstimate(
+            flops=10 ** 10 * n, bytes_accessed=3 * 10 ** 6 * n, transcendentals=3 * 10 ** 7 * n
+        ),
     )(tally, gas, mass, cosine, albedo, order, table, light)
 
-def padded(cells, sides, width, closed):
-    for axis, dim in sides:
-        count = lax.axis_size(axis)
-        ends = count if closed else count - 1
-        head = lax.slice_in_dim(cells, 0, width, axis=dim)
-        tail = lax.slice_in_dim(cells, cells.shape[dim] - width, cells.shape[dim], axis=dim)
-        cells = jnp.concatenate(
-            [
-                lax.ppermute(tail, axis, [(i, (i + 1) % count) for i in range(ends)]),
-                cells,
-                lax.ppermute(head, axis, [((i + 1) % count, i) for i in range(ends)]),
-            ],
-            axis=dim,
+
+def step(field, west, east, south, north, weights):
+    return (
+        field
+        + weights[0] * (west - field)
+        + weights[1] * (east - field)
+        + weights[2] * (south - field)
+        + weights[3] * (north - field)
+    )
+
+
+def march_kernel(own_ref, south_ref, north_ref, west_ref, east_ref, heat0_ref, heat1_ref, out_ref):
+    width = own_ref.shape[2]
+    rows = {-2: (south_ref, 0), -1: (south_ref, 1), 0: (own_ref, 0), 1: (own_ref, 1), 2: (north_ref, 0), 3: (north_ref, 1)}
+    middle = slice(HALO, HALO + width)
+
+    def plain(row, levels):
+        ref, at = rows[row]
+        return ref[levels, at, :]
+
+    def wide(row, levels):
+        return jnp.concatenate(
+            [west_ref[levels, row + 1, :], plain(row, levels), east_ref[levels, row + 1, :]], axis=1
         )
-    return cells
-
-
-def march_forward(thermal_field, zonal_weights, meridional_weights):
-    prognostic_field = thermal_field
-    for step_index in range(DSTEPS):
-        lon_rims = padded(prognostic_field, (("lon", 2),), 1, True)
-        lat_rims = padded(prognostic_field.astype(jnp.bfloat16), (("lat", 1),), 1, False).astype(
-            prognostic_field.dtype
-        )
-        western = lon_rims[:, :, :-2]
-        eastern = lon_rims[:, :, 2:]
-        southern = lat_rims[:, :-2, :]
-        northern = lat_rims[:, 2:, :]
-        prognostic_field = (
-            prognostic_field
-            + zonal_weights[0] * (western - prognostic_field)
-            + zonal_weights[1] * (eastern - prognostic_field)
-            + meridional_weights[0] * (southern - prognostic_field)
-            + meridional_weights[1] * (northern - prognostic_field)
-        )
-    return prognostic_field
+
+    def west_of(cells):
+        return pltpu.roll(cells, 1, 1)
+
+    def east_of(cells):
+        return pltpu.roll(cells, cells.shape[1] - 1, 1)
+
+    weights = {}
+    for row in (0, 1):
+        weights[row] = [wide(row, slice(TIERS + k, TIERS + k + 1)) for k in range(4)]
+    for row in (-1, 2):
+        weights[row] = [plain(row, slice(TIERS + k, TIERS + k + 1)) for k in range(4)]
+    chunk = 16
+
+    def levels_step(h, carry):
+        levels = pl.ds(pl.multiple_of(h * chunk, chunk), chunk)
+        first = {row: wide(row, levels) for row in (-1, 0, 1, 2)}
+        second = {}
+        for row in (0, 1):
+            f = first[row]
+            second[row] = step(f, west_of(f), east_of(f), first[row - 1], first[row + 1], weights[row])
+        for row in (-1, 2):
+            f = first[row]
+            south = plain(row - 1, levels) if row < 0 else first[row - 1][:, middle]
+            north = first[row + 1][:, middle] if row < 0 else plain(row + 1, levels)
+            second[row] = step(
+                f[:, middle], west_of(f)[:, middle], east_of(f)[:, middle], south, north, weights[row]
+            )
+        for row, heat_ref in ((0, heat0_ref), (1, heat1_ref)):
+            f = second[row]
+            south = second[row - 1] if row == 0 else second[row - 1][:, middle]
+            north = second[row + 1][:, middle] if row == 0 else second[row + 1]
+            third = step(
+                f[:, middle], west_of(f)[:, middle], east_of(f)[:, middle], south, north,
+                [w[:, middle] for w in weights[row]],
+            )
+            out_ref[levels, row, :] = third + heat_ref[0, levels, :]
+        return carry
+
+    lax.fori_loop(0, TIERS // chunk, levels_step, 0)
+
+
+def march(own, south, north, west, east, heat0, heat1):
+    return pl.pallas_call(
+        march_kernel,
+        out_shape=jax.ShapeDtypeStruct((TIERS, own.shape[1], own.shape[2]), jnp.float32),
+        compiler_params=pltpu.CompilerParams(vmem_limit_bytes=VMEM_BYTES),
+    )(own, south, north, west, east, heat0, heat1)
+
+
+def shifted(cells, axis, by, closed):
+    count = lax.axis_size(axis)
+    pairs = [(i, (i + by) % count) for i in range(count) if closed or 0 <= i + by < count]
+    return lax.ppermute(cells, axis, pairs)
 
 
 def per_device(
@@ -216,18 +280,31 @@
     daytime_tile_tally,
     daytime_tile_order,
 ):
-    prognostic_field = march_forward(thermal_field, zonal_weights, meridional_weights)
-    heat = radiation(
-        gas_burden,
-        tier_air_weight,
-        solar_elevation_factor,
-        ground_reflectance,
-        daytime_tile_order.reshape(1, -1),
-        extinction_table,
-        incoming_irradiance.reshape(1, -1),
-        daytime_tile_tally,
-    )
-    return prognostic_field + heat.transpose(1, 0, 2)
+    def heating(row, gas):
+        return radiation(
+            gas,
+            tier_air_weight,
+            solar_elevation_factor,
+            ground_reflectance,
+            daytime_tile_order.reshape(1, -1),
+            extinction_table,
+            incoming_irradiance.reshape(1, -1),
+            daytime_tile_tally,
+            rows=(row,),
+        )
+
+    own = jnp.concatenate([thermal_field, zonal_weights, meridional_weights], axis=0)
+    south = shifted(own, "lat", 1, False)
+    north = shifted(own, "lat", -1, False)
+    heat0 = heating(0, gas_burden)
+    south, north, heat0 = lax.optimization_barrier((south, north, heat0))
+    near = jnp.concatenate([south[:, 1:], own, north[:, :1]], axis=1)
+    last, first = near[:, :, -HALO:], near[:, :, :HALO]
+    gas_burden, last, first = lax.optimization_barrier((gas_burden, last, first))
+    west = shifted(last, "lon", 1, True)
+    east = shifted(first, "lon", -1, True)
+    heat1 = heating(1, gas_burden)
+    return march(own, south, north, west, east, heat0, heat1)
 
 
 def solution(mesh):

time: 88.2 us -> 70.5 us (0.80)
  starting transfers between devices: 28.3 us -> 14.3 us
  Pallas kernels: 42.4 us -> 49.8 us
  local copies, waits for them, and re-layouts: 10.3 us -> 4.38 us
  waiting for transfers between devices: 4.69 us -> 0.01 us
    ppermute x8 -> x4, starting transfers between devices: 28.3 us -> 14.3 us  [shifted(): return lax.ppermute(cells, axis, pairs)]
    unnamed x20 -> x12, local copies, waits for them, and re-layouts: 8.87 us -> 3.21 us
    ppermute x8 -> x4, waiting for transfers between devices: 4.69 us -> 0.01 us  [shifted(): return lax.ppermute(cells, axis, pairs)]
    pallas_call x0 -> x1, Pallas kernels: none -> 4.46 us  [march(): pl.pallas_call(march_kernel, out_shape=jax.ShapeDtypeStruct((TIERS, own.s...]
    pallas_call x1 -> x2, Pallas kernels: 42.4 us -> 45.3 us  [radiation(): pl.pallas_call(functools.partial(rad_kernel, rows), out_shape=jax.ShapeDt...]
    add x1 -> x0, local copies, waits for them, and re-layouts: 1.2 us -> none  [per_device(): return prognostic_field + heat.transpose(1, 0, 2)]
  transfers between devices with their start and end apart: 8 -> 4, of which waited for: 2 -> 0; matrix products, arithmetic and copies ran while one was open for 2% -> 0% of each run, Pallas kernels for 48% -> 65%
where the time goes in v2:
time: 70.5 us; the launch traced here: 69.7 us
  Pallas kernels  49.8 us (71%)
  starting transfers between devices  14.3 us (20%)
  local copies, waits for them, and re-layouts  4.38 us (6%)
  between operations  0.78 us (1%)
    pallas_call x2, Pallas kernels, radiation(): pl.pallas_call(functools.partial(rad_kernel, rows), out_shape=jax.ShapeDt...  45.3 us
    ppermute x4, starting transfers between devices, shifted(): return lax.ppermute(cells, axis, pairs)  14.3 us
    pallas_call x1, Pallas kernels, march(): pl.pallas_call(march_kernel, out_shape=jax.ShapeDtypeStruct((TIERS, own.s...  4.46 us
    unnamed x12, local copies, waits for them, and re-layouts  3.21 us
  transfers between devices with their start and end apart: 4, of which 0 were waited for; matrix products, arithmetic and copies ran while one was open for 0% of the time, Pallas kernels for 65%

profile of v2, /device:TPU:65, one launch (start us, length us, event | category | flops | bytes accessed | tf_op | source)
XLA Modules:
  0.0 69.7 jit_solution(9184255727592303240)
XLA Ops:
  0.0 1.1 %constant_dynamic-update-slice_fusion.2 = f32[132,2,512]{2,1,0:T(2,128)S(1)} fusion(f32[128,2,512]{2,1,0:T(2,128)} %param.11), kind=kLoop, calls=%fused_computation.5 | loop fusion | bytes 1048576
  1.1 0.7 %constant_dynamic-update-slice_fusion.1 = f32[132,2,512]{2,1,0:T(2,128)S(1)} fusion(f32[132,2,512]{2,1,0:T(2,128)S(1)} %constant_dynamic-update-slice_fusion.2, f32[2,2,512]{2,1,0:T(2,128)} %param.12), kind=kLoop, calls=%fused_computation.4 | loop fusion | bytes 16384
  1.8 0.7 %constant_dynamic-update-slice_fusion.own_ref = f32[132,2,512]{2,1,0:T(2,128)S(1)} fusion(f32[132,2,512]{2,1,0:T(2,128)S(1)} %constant_dynamic-update-slice_fusion.1, f32[2,2,512]{2,1,0:T(2,128)} %param.13), kind=kLoop, calls=%fused_computation.3 | loop fusion | bytes 16384 | tf_op jit(solution)/shard_map/concatenate | solution.py:296
  2.5 0.0 copy-start
  2.5 2.6 %collective-permute-start.1 = (f32[132,2,512]{2,1,0:T(2,128)S(1)}, f32[132,2,512]{2,1,0:T(2,128)S(1)}, u32[]{:S(2)}, u32[]{:S(2)}) collective-permute-start(f32[132,2,512]{2,1,0:T(2,128)S(1)} %constant_dynamic-update-slice_fusion.own_ref), channel_id=1, source_target_pairs={{1,0},{2,1},{3,2},{4,3},{5,4},{6,5},{7,6},{9,8},{10,9},{11,10},{12... | collective-permute-start | bytes 1622024 | tf_op jit(solution)/shard_map/ppermute | solution.py:267
  5.1 6.0 %collective-permute-start = (f32[132,2,512]{2,1,0:T(2,128)S(1)}, f32[132,2,512]{2,1,0:T(2,128)S(1)}, u32[]{:S(2)}, u32[]{:S(2)}) collective-permute-start(f32[132,2,512]{2,1,0:T(2,128)S(1)} %constant_dynamic-update-slice_fusion.own_ref), channel_id=1, source_target_pairs={{0,1},{1,2},{2,3},{3,4},{4,5},{5,6},{6,7},{8,9},{9,10},{10,11},{11... | collective-permute-start | bytes 1622024 | tf_op jit(solution)/shard_map/ppermute | solution.py:267
  11.7 22.7 %shard_map.109.heat0_ref = f32[1,128,512]{2,1,0:T(8,128)} custom-call(s32[1,1]{1,0:T(1,128)S(6)} %copy.14.tally_ref, bf16[2,512,2048]{2,1,0:T(8,128)(2,1)} %gas_hbm.2, bf16[2,512,128]{2,1,0:T(8,128)(2,1)} %mass_hbm.3, bf16[2,512]{1,0:T(2,128)(2,1)} %cos_ref.3, bf16[2,512]{1,0:T(2,128)(2,1)} %alb_ref.3, s32[1,256]{1,0:T(1,128)} %bitcast.2, ...), custom_call_target="tpu_custom_call" | custom-call | flops 10000000000 | bytes 3000000 | tf_op jit(solution)/shard_map/pallas_call | solution.py:160
  34.4 0.0 collective-permute-done.1.north_ref
  34.4 0.0 copy-start.1
  34.4 0.0 collective-permute-done.south_ref
  34.4 0.0 copy-start.2
  34.5 0.3 slice.12
  34.7 0.2 slice.13
  34.9 0.0 copy-done
  34.9 0.4 pad_maximum_fusion
  35.3 0.8 %collective-permute-start.2 = (f32[132,4,128]{2,1,0:T(4,128)S(1)}, f32[132,4,128]{2,1,0:T(4,128)S(1)}, u32[]{:S(2)}, u32[]{:S(2)}) collective-permute-start(f32[132,4,128]{2,1,0:T(4,128)S(1)} %get-tuple-element.13), channel_id=1, source_target_pairs={{0,8},{8,16},{16,24},{24,32},{32,40},{40,48},{48,56},{56,64},{64,7... | collective-permute-start | bytes 811016 | tf_op jit(solution)/shard_map/ppermute | solution.py:267
  36.1 4.9 %collective-permute-start.3 = (f32[132,4,128]{2,1,0:T(4,128)S(1)}, f32[132,4,128]{2,1,0:T(4,128)S(1)}, u32[]{:S(2)}, u32[]{:S(2)}) collective-permute-start(f32[132,4,128]{2,1,0:T(4,128)S(1)} %get-tuple-element.14), channel_id=1, source_target_pairs={{0,248},{8,0},{16,8},{24,16},{32,24},{40,32},{48,40},{56,48},{64,5... | collective-permute-start | bytes 811016 | tf_op jit(solution)/shard_map/ppermute | solution.py:267
  41.1 22.7 %shard_map.110.heat1_ref = f32[1,128,512]{2,1,0:T(8,128)} custom-call(s32[1,1]{1,0:T(1,128)S(6)} %copy.14.tally_ref, bf16[2,512,2048]{2,1,0:T(8,128)(2,1)} %gas_hbm.2, bf16[2,512,128]{2,1,0:T(8,128)(2,1)} %mass_hbm.3, bf16[2,512]{1,0:T(2,128)(2,1)} %cos_ref.3, bf16[2,512]{1,0:T(2,128)(2,1)} %alb_ref.3, s32[1,256]{1,0:T(1,128)} %bitcast.3, ...), custom_call_target="tpu_custom_call" | custom-call | flops 10000000000 | bytes 3000000 | tf_op jit(solution)/shard_map/pallas_call | solution.py:160
  63.8 0.0 copy-done.1
  63.8 0.0 copy-done.2
  63.8 0.0 collective-permute-done.2.west_ref
  63.8 0.0 copy-start.3
  63.8 0.0 collective-permute-done.3.east_ref
  63.8 0.7 copy-done.3
  64.5 0.0 copy-start.4
  64.5 0.7 %copy-done.4 = f32[132,4,128]{2,1,0:T(4,128)} copy-done((f32[132,4,128]{2,1,0:T(4,128)}, f32[132,4,128]{2,1,0:T(4,128)S(1)}, u32[]{:S(2)}) %copy-start.4) | copy-done | bytes 270360
  65.2 4.5 %shard_map.111 = f32[128,2,512]{2,1,0:T(2,128)} custom-call(f32[132,2,512]{2,1,0:T(2,128)} %copy-done, f32[132,2,512]{2,1,0:T(2,128)} %copy-done.2, f32[132,2,512]{2,1,0:T(2,128)} %copy-done.1, f32[132,4,128]{2,1,0:T(4,128)} %copy-done.3, f32[132,4,128]{2,1,0:T(4,128)} %copy-done.4, f32[1,128,512]{2,1,0:T(8,128)} %shard_map.109.heat0_ref, ...), custom_call_target="tpu_custom_call" | custom-call | tf_op jit(solution)/shard_map/pallas_call | solution.py:257
Async XLA Ops:
  2.5 32.4 %copy-start = (f32[132,2,512]{2,1,0:T(2,128)}, f32[132,2,512]{2,1,0:T(2,128)S(1)}, u32[]{:S(2)}) copy-start(f32[132,2,512]{2,1,0:T(2,128)S(1)} %constant_dynamic-update-slice_fusion.own_ref) | copy-start | bytes 1622020
  2.5 31.9 %collective-permute-start.1 = (f32[132,2,512]{2,1,0:T(2,128)S(1)}, f32[132,2,512]{2,1,0:T(2,128)S(1)}, u32[]{:S(2)}, u32[]{:S(2)}) collective-permute-start(f32[132,2,512]{2,1,0:T(2,128)S(1)} %constant_dynamic-update-slice_fusion.own_ref), channel_id=1, source_target_pairs={{1,0},{2,1},{3,2},{4,3},{5,4},{6,5},{7,6},{9,8},{10,9},{11,10},{12... | collective-permute-start | bytes 1622024 | tf_op jit(solution)/shard_map/ppermute | solution.py:267
  5.1 29.4 %collective-permute-start = (f32[132,2,512]{2,1,0:T(2,128)S(1)}, f32[132,2,512]{2,1,0:T(2,128)S(1)}, u32[]{:S(2)}, u32[]{:S(2)}) collective-permute-start(f32[132,2,512]{2,1,0:T(2,128)S(1)} %constant_dynamic-update-slice_fusion.own_ref), channel_id=1, source_target_pairs={{0,1},{1,2},{2,3},{3,4},{4,5},{5,6},{6,7},{8,9},{9,10},{10,11},{11... | collective-permute-start | bytes 1622024 | tf_op jit(solution)/shard_map/ppermute | solution.py:267
  34.4 29.3 %copy-start.1 = (f32[132,2,512]{2,1,0:T(2,128)}, f32[132,2,512]{2,1,0:T(2,128)S(1)}, u32[]{:S(2)}) copy-start(f32[132,2,512]{2,1,0:T(2,128)S(1)} %collective-permute-done.1.north_ref) | copy-start | bytes 1622020
  34.4 29.3 %copy-start.2 = (f32[132,2,512]{2,1,0:T(2,128)}, f32[132,2,512]{2,1,0:T(2,128)S(1)}, u32[]{:S(2)}) copy-start(f32[132,2,512]{2,1,0:T(2,128)S(1)} %collective-permute-done.south_ref) | copy-start | bytes 1622020
  35.3 28.5 %collective-permute-start.2 = (f32[132,4,128]{2,1,0:T(4,128)S(1)}, f32[132,4,128]{2,1,0:T(4,128)S(1)}, u32[]{:S(2)}, u32[]{:S(2)}) collective-permute-start(f32[132,4,128]{2,1,0:T(4,128)S(1)} %get-tuple-element.13), channel_id=1, source_target_pairs={{0,8},{8,16},{16,24},{24,32},{32,40},{40,48},{48,56},{56,64},{64,7... | collective-permute-start | bytes 811016 | tf_op jit(solution)/shard_map/ppermute | solution.py:267
  36.1 27.7 %collective-permute-start.3 = (f32[132,4,128]{2,1,0:T(4,128)S(1)}, f32[132,4,128]{2,1,0:T(4,128)S(1)}, u32[]{:S(2)}, u32[]{:S(2)}) collective-permute-start(f32[132,4,128]{2,1,0:T(4,128)S(1)} %get-tuple-element.14), channel_id=1, source_target_pairs={{0,248},{8,0},{16,8},{24,16},{32,24},{40,32},{48,40},{56,48},{64,5... | collective-permute-start | bytes 811016 | tf_op jit(solution)/shard_map/ppermute | solution.py:267
  63.8 0.7 %copy-start.3 = (f32[132,4,128]{2,1,0:T(4,128)}, f32[132,4,128]{2,1,0:T(4,128)S(1)}, u32[]{:S(2)}) copy-start(f32[132,4,128]{2,1,0:T(4,128)S(1)} %collective-permute-done.2.west_ref) | copy-start | bytes 811012
  64.5 0.7 %copy-start.4 = (f32[132,4,128]{2,1,0:T(4,128)}, f32[132,4,128]{2,1,0:T(4,128)S(1)}, u32[]{:S(2)}) copy-start(f32[132,4,128]{2,1,0:T(4,128)S(1)} %collective-permute-done.3.east_ref) | copy-start | bytes 811012

commit v3 on v2

v3 whole, which is shorter than its diff:
```python
import functools
import math

import jax
import jax.numpy as jnp
from jax import lax
from jax.experimental import pallas as pl
from jax.experimental.pallas import tpu as pltpu
from jax.sharding import PartitionSpec as P

DSTEPS = 2
DIFFUSE = 1.66
LOG2E = math.log2(math.e)
TIERS, TERMS, POINTS, BLOCK = 128, 16, 224, 4
RUN = 8
RUNS = TIERS // RUN
TILE = 256
ROWS = 8
LANES = 128
TOGETHER = 4
HALO = 128
ROWS_OF_LAT, HALVES = 2, 2
MIB = 1024 * 1024


def across(row, rows):
    return jnp.broadcast_to(row, (rows, row.shape[1]))


def halves(values):
    high = values.astype(jnp.bfloat16)
    low = (values - high.astype(jnp.float32)).astype(jnp.bfloat16)
    return jnp.concatenate([high, low], axis=1)


def thirds(values):
    high = values.astype(jnp.bfloat16)
    left = values - high.astype(jnp.float32)
    middle = left.astype(jnp.bfloat16)
    low = (left - middle.astype(jnp.float32)).astype(jnp.bfloat16)
    return high, middle, low


def by_rows(left, right):
    return lax.dot_general(left, right, (((1,), (1,)), ((), ())), preferred_element_type=jnp.float32)


def rad_kernel(tally_ref, gas_hbm, mass_hbm, cos_ref, alb_ref, order_ref, table_ref, light_ref, out_ref,
               lhs_ref, slope_ref, down_ref, up_ref, weight_ref, part_a, part_b, net_ref, whole_ref, light_log_ref, listed_ref,
               gas_ref, mass_ref, gas_sem, mass_sem):
    width = 2 * TILE

    def copies(row, half):
        cols = pl.ds(half * TILE, TILE)
        return (
            pltpu.make_async_copy(gas_hbm.at[row, cols], gas_ref.at[row, cols], gas_sem.at[row, half]),
            pltpu.make_async_copy(mass_hbm.at[row, cols], mass_ref.at[row, cols], mass_sem.at[row, half]),
        )

    for row in range(ROWS_OF_LAT):
        for half in range(HALVES):
            for copy in copies(row, half):
                copy.start()
    table = table_ref[...] * DIFFUSE
    table = jnp.concatenate([table, jnp.zeros((TERMS, 256 - POINTS), jnp.float32)], axis=1)
    stacked = jnp.concatenate([table] * RUN, axis=0).T[:POINTS]
    whole = halves(stacked * LOG2E)
    term = (lax.broadcasted_iota(jnp.int32, (1, 2 * LANES), 1) & (LANES - 1)) >> 4
    whole_wide = whole.astype(jnp.float32)
    for r in range(1, RUN + 1):
        chosen = jnp.where(term < r, whole_wide, 0.0)
        lhs_ref[(r - 1) * POINTS:r * POINTS, :] = chosen.astype(jnp.bfloat16)
    light = jnp.concatenate([light_ref[...], jnp.ones((1, 256 - POINTS), jnp.float32)], axis=1)
    light = across(jnp.log(light) * LOG2E, LANES).T[:POINTS]
    light_log_ref[...] = light
    whole_ref[...] = whole
    listed = across(order_ref[...].astype(jnp.float32), LANES).T
    rank = lax.broadcasted_iota(jnp.int32, listed.shape, 0)
    listed_ref[...] = jnp.where(rank < tally_ref[0, 0], listed, -1.0)

    def prepare(row, half):
        first = half * TILE
        cols = slice(first, first + TILE)

        def of_row(ref):
            both = ref[:, cols].astype(jnp.float32)
            return jnp.where(row == 0, both[0:1], both[1:2])

        cosine, albedo = of_row(cos_ref), of_row(alb_ref)
        slope = -1.0 / (DIFFUSE * cosine)
        slope_ref[half] = across(slope, ROWS)
        for copy in copies(row, half):
            copy.wait()
        amount = gas_ref[row, cols, 0:LANES].astype(jnp.float32)
        for b in range(1, RUNS):
            amount = amount + gas_ref[row, cols, b * LANES:(b + 1) * LANES].astype(jnp.float32)
        total = None
        for piece in thirds(amount):
            got = by_rows(whole_ref[...], jnp.concatenate([piece, piece], axis=1))
            total = got if total is None else total + got
        light = jnp.concatenate([light_log_ref[...]] * 2, axis=1)
        floor = light + (jnp.log(albedo) * LOG2E) + (slope - 1.0) * total
        down_ref[half] = light
        up_ref[half] = floor
        top = jnp.exp2(light) - jnp.exp2(floor)
        net_ref[half] = jnp.sum(top.reshape(POINTS // ROWS, ROWS, TILE), axis=0)
        eye = (lax.broadcasted_iota(jnp.int32, (LANES, LANES), 0)
               == lax.broadcasted_iota(jnp.int32, (LANES, LANES), 1)).astype(jnp.float32).astype(jnp.bfloat16)
        mass = by_rows(eye, mass_ref[row, cols, :])
        lit = []
        for t in range(TILE // LANES):
            block = (lax.broadcasted_iota(jnp.int32, (1, LANES), 1) + (row * width + first + t * LANES)) >> 2
            hit = jnp.where(listed_ref[...] == block.astype(jnp.float32), 1.0, 0.0)
            lit.append(jnp.sum(hit, axis=0, keepdims=True))
        lit = jnp.concatenate(lit, axis=1)
        weight_ref[half] = cosine * lit / mass

    def run_row(row, carry):
        for half in range(HALVES):
            prepare(row, half)

        def place(n):
            half, b = n >> 4, n & (RUNS - 1)
            return half, pl.multiple_of(half * TILE, TILE), b

        def parts(n):
            half, first, b = place(n)
            g = gas_ref[row, pl.ds(first, TILE), pl.ds(pl.multiple_of(b * LANES, LANES), LANES)]
            return by_rows(lhs_ref[...], jnp.concatenate([g, g], axis=1))

        def process(part_ref, n):
            half, first, b = place(n)
            levels = pl.ds(pl.multiple_of(b * RUN, RUN), RUN)
            for t in range(TILE // LANES):
                cols = slice(t * LANES, (t + 1) * LANES)
                s = slope_ref[half, :, cols]
                acc = [None] * (RUN + 1)
                for q in range(POINTS // ROWS):
                    here = slice(q * ROWS, (q + 1) * ROWS)
                    down0 = down_ref[half, here, cols]
                    up0 = up_ref[half, here, cols]
                    for r in range(1, RUN + 1):
                        at = (r - 1) * POINTS + q * ROWS
                        part = part_ref[at:at + ROWS, cols]
                        down = s * part + down0
                        up = part + up0
                        light = jnp.exp2(down)
                        acc[r] = (light if acc[r] is None else acc[r] + light) - jnp.exp2(up)
                    down_ref[half, here, cols] = down
                    up_ref[half, here, cols] = up
                acc[0] = net_ref[half, :, cols]
                net_ref[half, :, cols] = acc[RUN]
                diffs = []
                for r in range(1, RUN + 1):
                    diffs.append(jnp.sum(acc[r - 1] - acc[r], axis=0, keepdims=True))
                lanes = pl.ds(pl.multiple_of(first + t * LANES, LANES), LANES)
                out_ref[row, levels, lanes] = jnp.concatenate(diffs, axis=0) * weight_ref[half, levels, cols]

        part_a[...] = parts(0)

        def some_runs(h, carry):
            for u in range(TOGETHER):
                b = TOGETHER * h + u
                now, later = (part_a, part_b) if u % 2 == 0 else (part_b, part_a)
                later[...] = parts(jnp.minimum(b + 1, HALVES * RUNS - 1))
                process(now, b)
            return carry

        lax.fori_loop(0, HALVES * RUNS // TOGETHER, some_runs, 0)
        return carry

    lax.fori_loop(0, ROWS_OF_LAT, run_row, 0)


def radiation(gas, mass, cosine, albedo, order, table, light, tally):
    whole = lambda shape: pl.BlockSpec(shape, lambda: (0,) * len(shape))
    n, width = ROWS_OF_LAT, HALVES * TILE
    return pl.pallas_call(
        rad_kernel,
        out_shape=jax.ShapeDtypeStruct((n, TIERS, width), jnp.float32),
        in_specs=[
            pl.BlockSpec(memory_space=pltpu.SMEM),
            pl.BlockSpec(memory_space=pltpu.HBM),
            pl.BlockSpec(memory_space=pltpu.HBM),
            whole((n, width)), whole((n, width)), whole((1, 256)), whole((TERMS, POINTS)), whole((1, POINTS)),
        ],
        out_specs=whole((n, TIERS, width)),
        scratch_shapes=[
            pltpu.VMEM((RUN * POINTS, 2 * LANES), jnp.bfloat16),
            pltpu.VMEM((HALVES, ROWS, TILE), jnp.float32),
            pltpu.VMEM((HALVES, POINTS, TILE), jnp.float32),
            pltpu.VMEM((HALVES, POINTS, TILE), jnp.float32),
            pltpu.VMEM((HALVES, TIERS, TILE), jnp.float32),
            pltpu.VMEM((RUN * POINTS, TILE), jnp.float32),
            pltpu.VMEM((RUN * POINTS, TILE), jnp.float32),
            pltpu.VMEM((HALVES, ROWS, TILE), jnp.float32),
            pltpu.VMEM((POINTS, 2 * LANES), jnp.bfloat16),
            pltpu.VMEM((POINTS, LANES), jnp.float32),
            pltpu.VMEM((256, LANES), jnp.float32),
            pltpu.VMEM((n, width, TIERS * TERMS), jnp.bfloat16),
            pltpu.VMEM((n, width, TIERS), jnp.bfloat16),
            pltpu.SemaphoreType.DMA((n, HALVES)),
            pltpu.SemaphoreType.DMA((n, HALVES)),
        ],
        compiler_params=pltpu.CompilerParams(vmem_limit_bytes=60 * MIB),
        cost_estimate=pl.CostEstimate(flops=2 * 10 ** 10, bytes_accessed=6 * 10 ** 6, transcendentals=6 * 10 ** 7),
    )(tally, gas, mass, cosine, albedo, order, table, light)


def step(field, west, east, south, north, weights):
    return (
        field
        + weights[0] * (west - field)
        + weights[1] * (east - field)
        + weights[2] * (south - field)
        + weights[3] * (north - field)
    )


def copy_all(copies):
    for copy in copies:
        copy.start()
    for copy in copies:
        copy.wait()


def stacked_copies(sources, lanes, target, target_lanes, sems):
    copies, at = [], 0
    for k, source in enumerate(sources):
        depth = source.shape[0]
        copies.append(pltpu.make_async_copy(
            source.at[:, :, lanes], target.at[at:at + depth, :, target_lanes], sems.at[k]))
        at += depth
    return copies


def rims_kernel(field_ref, zonal_ref, meridional_ref, first_ref, last_ref, sems):
    width = field_ref.shape[2]
    sources = (field_ref, zonal_ref, meridional_ref)
    every = slice(0, HALO)
    copy_all(
        stacked_copies(sources, slice(0, HALO), first_ref, every, sems.at[0])
        + stacked_copies(sources, slice(width - HALO, width), last_ref, every, sems.at[1])
    )


def widened_kernel(field_ref, zonal_ref, meridional_ref, west_ref, east_ref, wide_ref, sems):
    width = field_ref.shape[2]
    copy_all(
        stacked_copies((field_ref, zonal_ref, meridional_ref), slice(0, width), wide_ref,
                       slice(HALO, HALO + width), sems.at[0])
        + stacked_copies((west_ref,), slice(0, HALO), wide_ref, slice(0, HALO), sems.at[1])
        + stacked_copies((east_ref,), slice(0, HALO), wide_ref, slice(HALO + width, HALO + width + HALO), sems.at[2])
    )


def moved(kernel, out_shape, groups, *arrays):
    anywhere = pl.BlockSpec(memory_space=pltpu.HBM)
    return pl.pallas_call(
        kernel,
        out_shape=out_shape,
        in_specs=[anywhere] * len(arrays),
        out_specs=jax.tree.map(lambda shape: anywhere, out_shape),
        scratch_shapes=[pltpu.SemaphoreType.DMA((groups, 3))],
        compiler_params=pltpu.CompilerParams(vmem_limit_bytes=60 * MIB),
    )(*arrays)


def march_kernel(own_ref, south_ref, north_ref, own_weights, south_weights, north_weights, heat_ref, out_ref):
    width = own_ref.shape[2] - 2 * HALO
    rows = {-2: (south_ref, 0), -1: (south_ref, 1), 0: (own_ref, 0), 1: (own_ref, 1), 2: (north_ref, 0), 3: (north_ref, 1)}
    of_row = {-1: (south_weights, 1), 0: (own_weights, 0), 1: (own_weights, 1), 2: (north_weights, 0)}
    middle = slice(HALO, HALO + width)

    def wide(row, levels):
        ref, at = rows[row]
        return ref[levels, at, :]

    def plain(row, levels):
        ref, at = rows[row]
        return ref[levels, at, middle]

    def west_of(cells):
        return pltpu.roll(cells, 1, 1)

    def east_of(cells):
        return pltpu.roll(cells, cells.shape[1] - 1, 1)

    weights = {}
    for row in (-1, 0, 1, 2):
        ref, at = of_row[row]
        lanes = slice(None) if row in (0, 1) else middle
        weights[row] = [ref[k:k + 1, at, lanes] for k in range(4)]
    chunk = 16

    def levels_step(h, carry):
        levels = pl.ds(pl.multiple_of(h * chunk, chunk), chunk)
        first = {row: wide(row, levels) for row in (-1, 0, 1, 2)}
        second = {}
        for row in (0, 1):
            f = first[row]
            second[row] = step(f, west_of(f), east_of(f), first[row - 1], first[row + 1], weights[row])
        for row in (-1, 2):
            f = first[row]
            south = plain(row - 1, levels) if row < 0 else first[row - 1][:, middle]
            north = first[row + 1][:, middle] if row < 0 else plain(row + 1, levels)
            second[row] = step(
                f[:, middle], west_of(f)[:, middle], east_of(f)[:, middle], south, north, weights[row]
            )
        for row in (0, 1):
            f = second[row]
            south = second[row - 1] if row == 0 else second[row - 1][:, middle]
            north = second[row + 1][:, middle] if row == 0 else second[row + 1]
            third = step(
                f[:, middle], west_of(f)[:, middle], east_of(f)[:, middle], south, north,
                [w[:, middle] for w in weights[row]],
            )
            out_ref[levels, row, :] = third + heat_ref[row, levels, :]
        return carry

    lax.fori_loop(0, heat_ref.shape[1] // chunk, levels_step, 0)


def march(own, south, north, heat):
    stripes, reach, width = own.shape[1], own.shape[2], heat.shape[2]
    deep = 32
    cells = pl.BlockSpec((deep, stripes, reach), lambda i: (i, 0, 0))
    weights = pl.BlockSpec((4, stripes, reach), lambda i: (TIERS // 4, 0, 0))
    return pl.pallas_call(
        march_kernel,
        grid=(TIERS // deep,),
        in_specs=[cells] * 3 + [weights] * 3 + [pl.BlockSpec((stripes, deep, width), lambda i: (0, i, 0))],
        out_specs=pl.BlockSpec((deep, stripes, width), lambda i: (i, 0, 0)),
        out_shape=jax.ShapeDtypeStruct((TIERS, stripes, width), jnp.float32),
        compiler_params=pltpu.CompilerParams(vmem_limit_bytes=60 * MIB),
    )(own, south, north, own, south, north, heat)


def shifted(cells, axis, by, closed):
    count = lax.axis_size(axis)
    pairs = [(i, (i + by) % count) for i in range(count) if closed or 0 <= i + by < count]
    return lax.ppermute(cells, axis, pairs)


def per_device(
    thermal_field,
    zonal_weights,
    meridional_weights,
    gas_burden,
    tier_air_weight,
    solar_elevation_factor,
    ground_reflectance,
    extinction_table,
    incoming_irradiance,
    daytime_tile_tally,
    daytime_tile_order,
):
    parts = (thermal_field, zonal_weights, meridional_weights)
    depth, stripes, width = TIERS + 4, thermal_field.shape[1], thermal_field.shape[2]
    rim = jax.ShapeDtypeStruct((depth, stripes, HALO), jnp.float32)
    first, last = moved(rims_kernel, (rim, rim), 2, *parts)
    west = shifted(last, "lon", 1, True)
    east = shifted(first, "lon", -1, True)
    broad = jax.ShapeDtypeStruct((depth, stripes, width + 2 * HALO), jnp.float32)
    own = moved(widened_kernel, broad, 3, *parts, west, east)
    own, gas_burden = lax.optimization_barrier((own, gas_burden))
    south = shifted(own, "lat", 1, False)
    north = shifted(own, "lat", -1, False)
    heat = radiation(
        gas_burden,
        tier_air_weight,
        solar_elevation_factor,
        ground_reflectance,
        daytime_tile_order.reshape(1, -1),
        extinction_table,
        incoming_irradiance.reshape(1, -1),
        daytime_tile_tally,
    )
    return march(own, south, north, heat)


def solution(mesh):
    placed = (
        P(None, "lat", "lon"),
        P(None, "lat", "lon"),
        P(None, "lat", "lon"),
        P("lat", "lon", None),
        P("lat", "lon", None),
        P("lat", "lon"),
        P("lat", "lon"),
        P(),
        P(),
        P("lat", "lon"),
        P("lat", "lon", None),
    )
    return jax.shard_map(
        per_device, mesh=mesh, in_specs=placed, out_specs=P(None, "lat", "lon"), check_vma=False
    )
```

time: 70.5 us -> 106 us (1.50)
  Pallas kernels: 49.8 us -> 82.7 us
  waiting for transfers between devices: 0.01 us -> 2.79 us
  starting transfers between devices: 14.3 us -> 16.1 us
  local copies, waits for them, and re-layouts: 4.38 us -> 3.11 us
    pallas_call x3 -> x4, Pallas kernels: 49.8 us -> 82.7 us  [the longest x1 42.7 us: radiation(): pl.pallas_call(rad_kernel, out_shape=jax.ShapeDtypeStruct((n, TIERS, widt...]
    ppermute x4, waiting for transfers between devices: 0.01 us -> 2.79 us  [shifted(): return lax.ppermute(cells, axis, pairs)]
    ppermute x4, starting transfers between devices: 14.3 us -> 16.1 us  [shifted(): return lax.ppermute(cells, axis, pairs)]
    unnamed x12 -> x8, local copies, waits for them, and re-layouts: 3.21 us -> 3.11 us
  transfers between devices with their start and end apart: 4 -> 4, of which waited for: 0 -> 1; matrix products, arithmetic and copies ran while one was open for 0% -> 0% of each run, Pallas kernels for 65% -> 40%
where the time goes in v3:
time: 106 us; the launch traced here: 105 us
  Pallas kernels  82.7 us (78%)
  starting transfers between devices  16.1 us (15%)
  local copies, waits for them, and re-layouts  3.11 us (3%)
  waiting for transfers between devices  2.79 us (3%)
    pallas_call x1, Pallas kernels, radiation(): pl.pallas_call(rad_kernel, out_shape=jax.ShapeDtypeStruct((n, TIERS, widt...  42.7 us
    pallas_call x2, Pallas kernels, moved(): pl.pallas_call(kernel, out_shape=out_shape, in_specs=[anywhere] * len(arr...  35.1 us
    ppermute x4, starting transfers between devices, shifted(): return lax.ppermute(cells, axis, pairs)  16.1 us
    pallas_call x1, Pallas kernels, march(): pl.pallas_call(march_kernel, grid=(TIERS // deep,), in_specs=[cells] * 3...  4.93 us
    unnamed x8, local copies, waits for them, and re-layouts  3.11 us
    ppermute x4, waiting for transfers between devices, shifted(): return lax.ppermute(cells, axis, pairs)  2.79 us
  transfers between devices with their start and end apart: 4, of which 1 were waited for; matrix products, arithmetic and copies ran while one was open for 0% of the time, Pallas kernels for 40%

profile of v3, /device:TPU:65, one launch (start us, length us, event | category | flops | bytes accessed | tf_op | source)
XLA Modules:
  0.0 105.5 jit_solution(14460798359579122873)
XLA Ops:
  0.0 9.3 %shard_map.109 = (f32[132,2,128]{2,1,0:T(2,128)}, f32[132,2,128]{2,1,0:T(2,128)}) custom-call(f32[128,2,512]{2,1,0:T(2,128)} %field_ref.3, f32[2,2,512]{2,1,0:T(2,128)} %zonal_ref.3, f32[2,2,512]{2,1,0:T(2,128)} %meridional_ref.3), custom_call_target="tpu_custom_call" | custom-call | tf_op jit(solution)/shard_map/pallas_call | solution.py:259
  9.3 1.7 %collective-permute-start = (f32[132,2,128]{2,1,0:T(2,128)}, f32[132,2,128]{2,1,0:T(2,128)S(1)}, u32[]{:S(2)}, u32[]{:S(2)}) collective-permute-start(f32[132,2,128]{2,1,0:T(2,128)} %get-tuple-element.9), channel_id=1, source_target_pairs={{0,8},{8,16},{16,24},{24,32},{32,40},{40,48},{48,56},{56,64},{64,7... | collective-permute-start | bytes 405512 | tf_op jit(solution)/shard_map/ppermute | solution.py:342
  11.1 4.7 %collective-permute-start.1 = (f32[132,2,128]{2,1,0:T(2,128)}, f32[132,2,128]{2,1,0:T(2,128)S(1)}, u32[]{:S(2)}, u32[]{:S(2)}) collective-permute-start(f32[132,2,128]{2,1,0:T(2,128)} %get-tuple-element.10), channel_id=1, source_target_pairs={{0,248},{8,0},{16,8},{24,16},{32,24},{40,32},{48,40},{56,48},{64,5... | collective-permute-start | bytes 405512 | tf_op jit(solution)/shard_map/ppermute | solution.py:342
  16.5 2.8 %collective-permute-done.west_ref = f32[132,2,128]{2,1,0:T(2,128)S(1)} collective-permute-done((f32[132,2,128]{2,1,0:T(2,128)}, f32[132,2,128]{2,1,0:T(2,128)S(1)}, u32[]{:S(2)}, u32[]{:S(2)}) %collective-permute-start) | collective-permute-done | bytes 135200 | tf_op jit(solution)/shard_map/ppermute | solution.py:342
  19.2 0.0 copy-start.2
  19.2 0.0 collective-permute-done.1.east_ref
  19.2 0.7 copy-done.2
  19.9 0.0 copy-start.3
  19.9 0.7 copy-done.3
  20.6 25.7 %shard_map.110.own_ref.own_weights = f32[132,2,768]{2,1,0:T(2,128)} custom-call(f32[128,2,512]{2,1,0:T(2,128)} %field_ref.3, f32[2,2,512]{2,1,0:T(2,128)} %zonal_ref.3, f32[2,2,512]{2,1,0:T(2,128)} %meridional_ref.3, f32[132,2,128]{2,1,0:T(2,128)} %copy-done.2, f32[132,2,128]{2,1,0:T(2,128)} %copy-done.3), custom_call_target="tpu_custom_call" | custom-call | tf_op jit(solution)/shard_map/pallas_call | solution.py:259
  46.3 4.0 %collective-permute-start.3 = (f32[132,2,768]{2,1,0:T(2,128)}, f32[132,2,768]{2,1,0:T(2,128)S(1)}, u32[]{:S(2)}, u32[]{:S(2)}) collective-permute-start(f32[132,2,768]{2,1,0:T(2,128)} %shard_map.110.own_ref.own_weights), channel_id=1, source_target_pairs={{1,0},{2,1},{3,2},{4,3},{5,4},{6,5},{7,6},{9,8},{10,9},{11,10},{12... | collective-permute-start | bytes 2433032 | tf_op jit(solution)/shard_map/ppermute | solution.py:342
  50.3 5.7 %collective-permute-start.2 = (f32[132,2,768]{2,1,0:T(2,128)}, f32[132,2,768]{2,1,0:T(2,128)S(1)}, u32[]{:S(2)}, u32[]{:S(2)}) collective-permute-start(f32[132,2,768]{2,1,0:T(2,128)} %shard_map.110.own_ref.own_weights), channel_id=1, source_target_pairs={{0,1},{1,2},{2,3},{3,4},{4,5},{5,6},{6,7},{8,9},{9,10},{10,11},{11... | collective-permute-start | bytes 2433032 | tf_op jit(solution)/shard_map/ppermute | solution.py:342
  56.0 42.7 %shard_map.111.heat_ref = f32[2,128,512]{2,1,0:T(8,128)} custom-call(s32[1,1]{1,0:T(1,128)S(6)} %copy.12.tally_ref, bf16[2,512,2048]{2,1,0:T(8,128)(2,1)} %gas_hbm, bf16[2,512,128]{2,1,0:T(8,128)(2,1)} %mass_hbm.1, bf16[2,512]{1,0:T(2,128)(2,1)} %cos_ref.1, bf16[2,512]{1,0:T(2,128)(2,1)} %alb_ref.1, s32[1,256]{1,0:T(1,128)} %bitcast.2, f32[16,224]{1,0:T(8,128)} %table_ref.1, ...), custom_call_target="tpu_custom_call" | custom-call | flops 20000000000 | bytes 6000000 | tf_op jit(solution)/shard_map/pallas_call | solution.py:178
  98.7 0.0 collective-permute-done.3.north_ref.north_weights
  98.7 0.0 copy-start
  98.7 0.0 collective-permute-done.2.south_ref.south_weights
  98.7 0.9 copy-done
  99.6 0.0 copy-start.1
  99.6 0.9 copy-done.1
  100.5 4.9 %shard_map.112 = f32[128,2,512]{2,1,0:T(2,128)} custom-call(f32[132,2,768]{2,1,0:T(2,128)} %shard_map.110.own_ref.own_weights, f32[132,2,768]{2,1,0:T(2,128)} %copy-done.1, f32[132,2,768]{2,1,0:T(2,128)} %copy-done, f32[132,2,768]{2,1,0:T(2,128)} %shard_map.110.own_ref.own_weights, f32[132,2,768]{2,1,0:T(2,128)} %copy-done.1, f32[132,2,768]{2,1,0:T(2,128)} %copy-done, ...), custom_call_target="tpu_custom_call" | custom-call | tf_op jit(solution)/shard_map/pallas_call | solution.py:329
Async XLA Ops:
  9.3 9.9 %collective-permute-start = (f32[132,2,128]{2,1,0:T(2,128)}, f32[132,2,128]{2,1,0:T(2,128)S(1)}, u32[]{:S(2)}, u32[]{:S(2)}) collective-permute-start(f32[132,2,128]{2,1,0:T(2,128)} %get-tuple-element.9), channel_id=1, source_target_pairs={{0,8},{8,16},{16,24},{24,32},{32,40},{40,48},{48,56},{56,64},{64,7... | collective-permute-start | bytes 405512 | tf_op jit(solution)/shard_map/ppermute | solution.py:342
  11.1 8.2 %collective-permute-start.1 = (f32[132,2,128]{2,1,0:T(2,128)}, f32[132,2,128]{2,1,0:T(2,128)S(1)}, u32[]{:S(2)}, u32[]{:S(2)}) collective-permute-start(f32[132,2,128]{2,1,0:T(2,128)} %get-tuple-element.10), channel_id=1, source_target_pairs={{0,248},{8,0},{16,8},{24,16},{32,24},{40,32},{48,40},{56,48},{64,5... | collective-permute-start | bytes 405512 | tf_op jit(solution)/shard_map/ppermute | solution.py:342
  19.2 0.7 copy-start.2
  19.9 0.7 copy-start.3
  46.3 52.4 %collective-permute-start.3 = (f32[132,2,768]{2,1,0:T(2,128)}, f32[132,2,768]{2,1,0:T(2,128)S(1)}, u32[]{:S(2)}, u32[]{:S(2)}) collective-permute-start(f32[132,2,768]{2,1,0:T(2,128)} %shard_map.110.own_ref.own_weights), channel_id=1, source_target_pairs={{1,0},{2,1},{3,2},{4,3},{5,4},{6,5},{7,6},{9,8},{10,9},{11,10},{12... | collective-permute-start | bytes 2433032 | tf_op jit(solution)/shard_map/ppermute | solution.py:342
  50.3 48.5 %collective-permute-start.2 = (f32[132,2,768]{2,1,0:T(2,128)}, f32[132,2,768]{2,1,0:T(2,128)S(1)}, u32[]{:S(2)}, u32[]{:S(2)}) collective-permute-start(f32[132,2,768]{2,1,0:T(2,128)} %shard_map.110.own_ref.own_weights), channel_id=1, source_target_pairs={{0,1},{1,2},{2,3},{3,4},{4,5},{5,6},{6,7},{8,9},{9,10},{10,11},{11... | collective-permute-start | bytes 2433032 | tf_op jit(solution)/shard_map/ppermute | solution.py:342
  98.7 0.9 copy-start
  99.6 0.9 copy-start.1

commit v4 on v2

v4 whole, which is shorter than its diff:
```python
import functools
import math

import jax
import jax.numpy as jnp
from jax import lax
from jax.experimental import pallas as pl
from jax.experimental.pallas import tpu as pltpu
from jax.sharding import PartitionSpec as P

DSTEPS = 2
DIFFUSE = 1.66
LOG2E = math.log2(math.e)
TIERS, TERMS, POINTS, BLOCK = 128, 16, 224, 4
RUN = 8
RUNS = TIERS // RUN
TILE = 256
ROWS = 8
LANES = 128
TOGETHER = 4
HALO = 128
ROWS_OF_LAT, HALVES = 2, 2
MIB = 1024 * 1024
MARCH_MIB = 50


def across(row, rows):
    return jnp.broadcast_to(row, (rows, row.shape[1]))


def halves(values):
    high = values.astype(jnp.bfloat16)
    low = (values - high.astype(jnp.float32)).astype(jnp.bfloat16)
    return jnp.concatenate([high, low], axis=1)


def thirds(values):
    high = values.astype(jnp.bfloat16)
    left = values - high.astype(jnp.float32)
    middle = left.astype(jnp.bfloat16)
    low = (left - middle.astype(jnp.float32)).astype(jnp.bfloat16)
    return high, middle, low


def by_rows(left, right):
    return lax.dot_general(left, right, (((1,), (1,)), ((), ())), preferred_element_type=jnp.float32)


def rad_kernel(row, tally_ref, gas_hbm, mass_hbm, cos_ref, alb_ref, order_ref, table_ref, light_ref, out_ref,
               lhs_ref, slope_ref, down_ref, up_ref, weight_ref, part_a, part_b, net_ref, whole_ref, light_log_ref, listed_ref,
               gas_ref, mass_ref, gas_sem, mass_sem):
    width = 2 * TILE

    def copies(half):
        cols = pl.ds(half * TILE, TILE)
        return (
            pltpu.make_async_copy(gas_hbm.at[row, cols], gas_ref.at[cols], gas_sem.at[half]),
            pltpu.make_async_copy(mass_hbm.at[row, cols], mass_ref.at[cols], mass_sem.at[half]),
        )

    for half in range(HALVES):
        for copy in copies(half):
            copy.start()
    table = table_ref[...] * DIFFUSE
    table = jnp.concatenate([table, jnp.zeros((TERMS, 256 - POINTS), jnp.float32)], axis=1)
    stacked = jnp.concatenate([table] * RUN, axis=0).T[:POINTS]
    whole = halves(stacked * LOG2E)
    term = (lax.broadcasted_iota(jnp.int32, (1, 2 * LANES), 1) & (LANES - 1)) >> 4
    whole_wide = whole.astype(jnp.float32)
    for r in range(1, RUN + 1):
        chosen = jnp.where(term < r, whole_wide, 0.0)
        lhs_ref[(r - 1) * POINTS:r * POINTS, :] = chosen.astype(jnp.bfloat16)
    light = jnp.concatenate([light_ref[...], jnp.ones((1, 256 - POINTS), jnp.float32)], axis=1)
    light = across(jnp.log(light) * LOG2E, LANES).T[:POINTS]
    light_log_ref[...] = light
    whole_ref[...] = whole
    listed = across(order_ref[...].astype(jnp.float32), LANES).T
    rank = lax.broadcasted_iota(jnp.int32, listed.shape, 0)
    listed_ref[...] = jnp.where(rank < tally_ref[0, 0], listed, -1.0)

    def prepare(half):
        first = half * TILE
        cols = slice(first, first + TILE)

        def of_row(ref):
            return ref[:, cols].astype(jnp.float32)[row:row + 1]

        cosine, albedo = of_row(cos_ref), of_row(alb_ref)
        slope = -1.0 / (DIFFUSE * cosine)
        slope_ref[half] = across(slope, ROWS)
        for copy in copies(half):
            copy.wait()
        amount = gas_ref[cols, 0:LANES].astype(jnp.float32)
        for b in range(1, RUNS):
            amount = amount + gas_ref[cols, b * LANES:(b + 1) * LANES].astype(jnp.float32)
        total = None
        for piece in thirds(amount):
            got = by_rows(whole_ref[...], jnp.concatenate([piece, piece], axis=1))
            total = got if total is None else total + got
        light = jnp.concatenate([light_log_ref[...]] * 2, axis=1)
        floor = light + (jnp.log(albedo) * LOG2E) + (slope - 1.0) * total
        down_ref[half] = light
        up_ref[half] = floor
        top = jnp.exp2(light) - jnp.exp2(floor)
        net_ref[half] = jnp.sum(top.reshape(POINTS // ROWS, ROWS, TILE), axis=0)
        eye = (lax.broadcasted_iota(jnp.int32, (LANES, LANES), 0)
               == lax.broadcasted_iota(jnp.int32, (LANES, LANES), 1)).astype(jnp.float32).astype(jnp.bfloat16)
        mass = by_rows(eye, mass_ref[cols, :])
        lit = []
        for t in range(TILE // LANES):
            block = (lax.broadcasted_iota(jnp.int32, (1, LANES), 1) + (row * width + first + t * LANES)) >> 2
            hit = jnp.where(listed_ref[...] == block.astype(jnp.float32), 1.0, 0.0)
            lit.append(jnp.sum(hit, axis=0, keepdims=True))
        lit = jnp.concatenate(lit, axis=1)
        weight_ref[half] = cosine * lit / mass

    for half in range(HALVES):
        prepare(half)

    def place(n):
        half, b = n >> 4, n & (RUNS - 1)
        return half, pl.multiple_of(half * TILE, TILE), b

    def parts(n):
        half, first, b = place(n)
        g = gas_ref[pl.ds(first, TILE), pl.ds(pl.multiple_of(b * LANES, LANES), LANES)]
        return by_rows(lhs_ref[...], jnp.concatenate([g, g], axis=1))

    def process(part_ref, n):
        half, first, b = place(n)
        levels = pl.ds(pl.multiple_of(b * RUN, RUN), RUN)
        for t in range(TILE // LANES):
            cols = slice(t * LANES, (t + 1) * LANES)
            s = slope_ref[half, :, cols]
            acc = [None] * (RUN + 1)
            for q in range(POINTS // ROWS):
                here = slice(q * ROWS, (q + 1) * ROWS)
                down0 = down_ref[half, here, cols]
                up0 = up_ref[half, here, cols]
                for r in range(1, RUN + 1):
                    at = (r - 1) * POINTS + q * ROWS
                    part = part_ref[at:at + ROWS, cols]
                    down = s * part + down0
                    up = part + up0
                    light = jnp.exp2(down)
                    acc[r] = (light if acc[r] is None else acc[r] + light) - jnp.exp2(up)
                down_ref[half, here, cols] = down
                up_ref[half, here, cols] = up
            acc[0] = net_ref[half, :, cols]
            net_ref[half, :, cols] = acc[RUN]
            diffs = []
            for r in range(1, RUN + 1):
                diffs.append(jnp.sum(acc[r - 1] - acc[r], axis=0, keepdims=True))
            lanes = pl.ds(pl.multiple_of(first + t * LANES, LANES), LANES)
            out_ref[levels, lanes] = jnp.concatenate(diffs, axis=0) * weight_ref[half, levels, cols]

    part_a[...] = parts(0)

    def some_runs(h, carry):
        for u in range(TOGETHER):
            b = TOGETHER * h + u
            now, later = (part_a, part_b) if u % 2 == 0 else (part_b, part_a)
            later[...] = parts(jnp.minimum(b + 1, HALVES * RUNS - 1))
            process(now, b)
        return carry

    lax.fori_loop(0, HALVES * RUNS // TOGETHER, some_runs, 0)


def radiation(gas, mass, cosine, albedo, order, table, light, tally, row):
    whole = lambda shape: pl.BlockSpec(shape, lambda: (0,) * len(shape))
    n, width = ROWS_OF_LAT, HALVES * TILE
    return pl.pallas_call(
        functools.partial(rad_kernel, row),
        out_shape=jax.ShapeDtypeStruct((TIERS, width), jnp.float32),
        in_specs=[
            pl.BlockSpec(memory_space=pltpu.SMEM),
            pl.BlockSpec(memory_space=pltpu.HBM),
            pl.BlockSpec(memory_space=pltpu.HBM),
            whole((n, width)), whole((n, width)), whole((1, 256)), whole((TERMS, POINTS)), whole((1, POINTS)),
        ],
        out_specs=whole((TIERS, width)),
        scratch_shapes=[
            pltpu.VMEM((RUN * POINTS, 2 * LANES), jnp.bfloat16),
            pltpu.VMEM((HALVES, ROWS, TILE), jnp.float32),
            pltpu.VMEM((HALVES, POINTS, TILE), jnp.float32),
            pltpu.VMEM((HALVES, POINTS, TILE), jnp.float32),
            pltpu.VMEM((HALVES, TIERS, TILE), jnp.float32),
            pltpu.VMEM((RUN * POINTS, TILE), jnp.float32),
            pltpu.VMEM((RUN * POINTS, TILE), jnp.float32),
            pltpu.VMEM((HALVES, ROWS, TILE), jnp.float32),
            pltpu.VMEM((POINTS, 2 * LANES), jnp.bfloat16),
            pltpu.VMEM((POINTS, LANES), jnp.float32),
            pltpu.VMEM((256, LANES), jnp.float32),
            pltpu.VMEM((width, TIERS * TERMS), jnp.bfloat16),
            pltpu.VMEM((width, TIERS), jnp.bfloat16),
            pltpu.SemaphoreType.DMA((HALVES,)),
            pltpu.SemaphoreType.DMA((HALVES,)),
        ],
        compiler_params=pltpu.CompilerParams(vmem_limit_bytes=60 * MIB),
        cost_estimate=pl.CostEstimate(flops=2 * 10 ** 10, bytes_accessed=6 * 10 ** 6, transcendentals=6 * 10 ** 7),
    )(tally, gas, mass, cosine, albedo, order, table, light)


def step(field, west, east, south, north, weights):
    return (
        field
        + weights[0] * (west - field)
        + weights[1] * (east - field)
        + weights[2] * (south - field)
        + weights[3] * (north - field)
    )


DEPTH = TIERS + 8


def gathered_kernel(field_ref, zonal_ref, meridional_ref, own_ref):
    for row in range(ROWS_OF_LAT):
        own_ref[row, 0:TIERS, :] = field_ref[:, row, :]
        weights = [ref[k:k + 1, row, :] for ref in (zonal_ref, meridional_ref) for k in range(2)]
        own_ref[row, TIERS:DEPTH, :] = jnp.concatenate(weights + weights, axis=0)


def gathered(field, zonal, meridional):
    return pl.pallas_call(
        gathered_kernel,
        out_shape=jax.ShapeDtypeStruct((ROWS_OF_LAT, DEPTH, field.shape[2]), jnp.float32),
        compiler_params=pltpu.CompilerParams(vmem_limit_bytes=60 * MIB),
    )(field, zonal, meridional)


def march_kernel(own_ref, south_ref, north_ref, west_ref, east_ref, heat0_ref, heat1_ref, out_ref):
    width = own_ref.shape[2]
    rows = {-2: (south_ref, 0), -1: (south_ref, 1), 0: (own_ref, 0), 1: (own_ref, 1), 2: (north_ref, 0), 3: (north_ref, 1)}
    middle = slice(HALO, HALO + width)

    def plain(row, levels):
        ref, at = rows[row]
        return ref[at, levels, :]

    def wide(row, levels):
        return jnp.concatenate(
            [west_ref[row + 1, levels, :], plain(row, levels), east_ref[row + 1, levels, :]], axis=1
        )

    def west_of(cells):
        return pltpu.roll(cells, 1, 1)

    def east_of(cells):
        return pltpu.roll(cells, cells.shape[1] - 1, 1)

    weights = {}
    for row in (-1, 0, 1, 2):
        load = wide if row in (0, 1) else plain
        weights[row] = [load(row, slice(TIERS + k, TIERS + k + 1)) for k in range(4)]
    chunk = 16

    def levels_step(h, carry):
        levels = pl.ds(pl.multiple_of(h * chunk, chunk), chunk)
        first = {row: wide(row, levels) for row in (-1, 0, 1, 2)}
        second = {}
        for row in (0, 1):
            f = first[row]
            second[row] = step(f, west_of(f), east_of(f), first[row - 1], first[row + 1], weights[row])
        for row in (-1, 2):
            f = first[row]
            south = plain(row - 1, levels) if row < 0 else first[row - 1][:, middle]
            north = first[row + 1][:, middle] if row < 0 else plain(row + 1, levels)
            second[row] = step(
                f[:, middle], west_of(f)[:, middle], east_of(f)[:, middle], south, north, weights[row]
            )
        for row, heat_ref in ((0, heat0_ref), (1, heat1_ref)):
            f = second[row]
            south = second[row - 1] if row == 0 else second[row - 1][:, middle]
            north = second[row + 1][:, middle] if row == 0 else second[row + 1]
            third = step(
                f[:, middle], west_of(f)[:, middle], east_of(f)[:, middle], south, north,
                [w[:, middle] for w in weights[row]],
            )
            out_ref[levels, row, :] = third + heat_ref[levels, :]
        return carry

    lax.fori_loop(0, TIERS // chunk, levels_step, 0)


def march(own, south, north, west, east, heat0, heat1):
    return pl.pallas_call(
        march_kernel,
        out_shape=jax.ShapeDtypeStruct((TIERS, ROWS_OF_LAT, own.shape[2]), jnp.float32),
        compiler_params=pltpu.CompilerParams(vmem_limit_bytes=MARCH_MIB * MIB),
    )(own, south, north, west, east, heat0, heat1)


def shifted(cells, axis, by, closed):
    count = lax.axis_size(axis)
    pairs = [(i, (i + by) % count) for i in range(count) if closed or 0 <= i + by < count]
    return lax.ppermute(cells, axis, pairs)


def per_device(
    thermal_field,
    zonal_weights,
    meridional_weights,
    gas_burden,
    tier_air_weight,
    solar_elevation_factor,
    ground_reflectance,
    extinction_table,
    incoming_irradiance,
    daytime_tile_tally,
    daytime_tile_order,
):
    def heating(row, gas):
        return radiation(
            gas,
            tier_air_weight,
            solar_elevation_factor,
            ground_reflectance,
            daytime_tile_order.reshape(1, -1),
            extinction_table,
            incoming_irradiance.reshape(1, -1),
            daytime_tile_tally,
            row,
        )

    own = gathered(thermal_field, zonal_weights, meridional_weights)
    south = shifted(own, "lat", 1, False)
    north = shifted(own, "lat", -1, False)
    heat0 = heating(0, gas_burden)
    south, north, heat0 = lax.optimization_barrier((south, north, heat0))
    near = jnp.concatenate([south[1:], own, north[:1]], axis=0)
    last, first = near[:, :, -HALO:], near[:, :, :HALO]
    gas_burden, last, first = lax.optimization_barrier((gas_burden, last, first))
    west = shifted(last, "lon", 1, True)
    east = shifted(first, "lon", -1, True)
    heat1 = heating(1, gas_burden)
    return march(own, south, north, west, east, heat0, heat1)


def solution(mesh):
    placed = (
        P(None, "lat", "lon"),
        P(None, "lat", "lon"),
        P(None, "lat", "lon"),
        P("lat", "lon", None),
        P("lat", "lon", None),
        P("lat", "lon"),
        P("lat", "lon"),
        P(),
        P(),
        P("lat", "lon"),
        P("lat", "lon", None),
    )
    return jax.shard_map(
        per_device, mesh=mesh, in_specs=placed, out_specs=P(None, "lat", "lon"), check_vma=False
    )
```

time: 70.5 us -> 66.6 us (0.945)
  local copies, waits for them, and re-layouts: 4.38 us -> 0.99 us
    unnamed x12 -> x6, local copies, waits for them, and re-layouts: 3.21 us -> 0.95 us
    pallas_call x3 -> x4, Pallas kernels: 49.8 us -> 49.8 us  [the longest x2 45.2 us: radiation(): pl.pallas_call(functools.partial(rad_kernel, row), out_shape=jax.ShapeDty...]
  transfers between devices with their start and end apart: 4 -> 4, of which waited for: 0 -> 0; matrix products, arithmetic and copies ran while one was open for 0% -> 0% of each run, Pallas kernels for 65% -> 68%
where the time goes in v4:
time: 66.6 us; the launch traced here: 66 us
  Pallas kernels  49.8 us (75%)
  starting transfers between devices  14.3 us (21%)
  local copies, waits for them, and re-layouts  0.99 us (1%)
  between operations  0.78 us (1%)
    pallas_call x2, Pallas kernels, radiation(): pl.pallas_call(functools.partial(rad_kernel, row), out_shape=jax.ShapeDty...  45.2 us
    ppermute x4, starting transfers between devices, shifted(): return lax.ppermute(cells, axis, pairs)  14.3 us
    pallas_call x1, Pallas kernels, march(): pl.pallas_call(march_kernel, out_shape=jax.ShapeDtypeStruct((TIERS, ROWS_...  2.68 us
    pallas_call x1, Pallas kernels, gathered(): pl.pallas_call(gathered_kernel, out_shape=jax.ShapeDtypeStruct((ROWS_OF_L...  1.97 us
  transfers between devices with their start and end apart: 4, of which 0 were waited for; matrix products, arithmetic and copies ran while one was open for 0% of the time, Pallas kernels for 68%

profile of v4, /device:TPU:65, one launch (start us, length us, event | category | flops | bytes accessed | tf_op | source)
XLA Modules:
  0.0 66.0 jit_solution(15007821200039943063)
XLA Ops:
  0.0 2.0 %shard_map.109.own_ref = f32[2,136,512]{2,1,0:T(8,128)} custom-call(f32[128,2,512]{2,1,0:T(2,128)} %field_ref.1, f32[2,2,512]{2,1,0:T(2,128)} %zonal_ref.1, f32[2,2,512]{2,1,0:T(2,128)} %meridional_ref.1), custom_call_target="tpu_custom_call" | custom-call | tf_op jit(solution)/shard_map/pallas_call | solution.py:226
  2.0 2.6 %collective-permute-start.1 = (f32[2,136,512]{2,1,0:T(8,128)}, f32[2,136,512]{2,1,0:T(8,128)S(1)}, u32[]{:S(2)}, u32[]{:S(2)}) collective-permute-start(f32[2,136,512]{2,1,0:T(8,128)} %shard_map.109.own_ref), channel_id=1, source_target_pairs={{1,0},{2,1},{3,2},{4,3},{5,4},{6,5},{7,6},{9,8},{10,9},{11,10},{12... | collective-permute-start | bytes 1671176 | tf_op jit(solution)/shard_map/ppermute | solution.py:298
  4.6 6.0 %collective-permute-start = (f32[2,136,512]{2,1,0:T(8,128)}, f32[2,136,512]{2,1,0:T(8,128)S(1)}, u32[]{:S(2)}, u32[]{:S(2)}) collective-permute-start(f32[2,136,512]{2,1,0:T(8,128)} %shard_map.109.own_ref), channel_id=1, source_target_pairs={{0,1},{1,2},{2,3},{3,4},{4,5},{5,6},{6,7},{8,9},{9,10},{10,11},{11... | collective-permute-start | bytes 1671176 | tf_op jit(solution)/shard_map/ppermute | solution.py:298
  11.2 0.0 copy-start
  11.2 22.6 %shard_map.110.heat0_ref = f32[128,512]{1,0:T(8,128)} custom-call(s32[1,1]{1,0:T(1,128)S(6)} %copy.12.tally_ref, bf16[2,512,2048]{2,1,0:T(8,128)(2,1)} %gas_hbm.2, bf16[2,512,128]{2,1,0:T(8,128)(2,1)} %mass_hbm.3, bf16[2,512]{1,0:T(2,128)(2,1)} %cos_ref.3, bf16[2,512]{1,0:T(2,128)(2,1)} %alb_ref.3, s32[1,256]{1,0:T(1,128)} %bitcast.2, f32[16,224]{1,0:T(8,128)} %table_ref.3, ...), custom_call_target="tpu_custom_call" | custom-call | flops 20000000000 | bytes 6000000 | tf_op jit(solution)/shard_map/pallas_call | solution.py:173
  33.9 0.0 collective-permute-done.1.north_ref
  33.9 0.0 collective-permute-done.south_ref
  33.9 0.0 copy-done
  34.0 0.0 copy-start.1
  34.0 0.8 %collective-permute-start.2 = (f32[4,136,128]{2,1,0:T(8,128)S(1)}, f32[4,136,128]{2,1,0:T(8,128)S(1)}, u32[]{:S(2)}, u32[]{:S(2)}) collective-permute-start(f32[4,136,128]{2,1,0:T(8,128)S(1)} %get-tuple-element.13), channel_id=1, source_target_pairs={{0,8},{8,16},{16,24},{24,32},{32,40},{40,48},{48,56},{56,64},{64,7... | collective-permute-start | bytes 835592 | tf_op jit(solution)/shard_map/ppermute | solution.py:298
  34.8 5.0 %collective-permute-start.3 = (f32[4,136,128]{2,1,0:T(8,128)S(1)}, f32[4,136,128]{2,1,0:T(8,128)S(1)}, u32[]{:S(2)}, u32[]{:S(2)}) collective-permute-start(f32[4,136,128]{2,1,0:T(8,128)S(1)} %get-tuple-element.14), channel_id=1, source_target_pairs={{0,248},{8,0},{16,8},{24,16},{32,24},{40,32},{48,40},{56,48},{64,5... | collective-permute-start | bytes 835592 | tf_op jit(solution)/shard_map/ppermute | solution.py:298
  39.8 22.6 %shard_map.111.heat1_ref = f32[128,512]{1,0:T(8,128)} custom-call(s32[1,1]{1,0:T(1,128)S(6)} %copy.12.tally_ref, bf16[2,512,2048]{2,1,0:T(8,128)(2,1)} %gas_hbm.2, bf16[2,512,128]{2,1,0:T(8,128)(2,1)} %mass_hbm.3, bf16[2,512]{1,0:T(2,128)(2,1)} %cos_ref.3, bf16[2,512]{1,0:T(2,128)(2,1)} %alb_ref.3, s32[1,256]{1,0:T(1,128)} %bitcast.3, f32[16,224]{1,0:T(8,128)} %table_ref.3, ...), custom_call_target="tpu_custom_call" | custom-call | flops 20000000000 | bytes 6000000 | tf_op jit(solution)/shard_map/pallas_call | solution.py:173
  62.3 0.0 collective-permute-done.2.west_ref
  62.3 0.0 collective-permute-done.3.east_ref
  62.4 0.0 copy-done.1
  62.4 0.0 copy-start.2
  62.4 0.9 %copy-done.2 = f32[128,512]{1,0:T(8,128)S(1)} copy-done((f32[128,512]{1,0:T(8,128)S(1)}, f32[128,512]{1,0:T(8,128)}, u32[]{:S(2)}) %copy-start.2) | copy-done | bytes 262168
  63.3 2.7 %shard_map.112 = f32[128,2,512]{2,1,0:T(2,128)} custom-call(f32[2,136,512]{2,1,0:T(8,128)S(1)} %copy-done, f32[2,136,512]{2,1,0:T(8,128)S(1)} %collective-permute-done.south_ref, f32[2,136,512]{2,1,0:T(8,128)S(1)} %collective-permute-done.1.north_ref, f32[4,136,128]{2,1,0:T(8,128)S(1)} %collective-permute-done.2.west_ref, ...), custom_call_target="tpu_custom_call" | custom-call | tf_op jit(solution)/shard_map/pallas_call | solution.py:288
  (3 shorter events, 0.1 us)
Async XLA Ops:
  2.0 31.9 %collective-permute-start.1 = (f32[2,136,512]{2,1,0:T(8,128)}, f32[2,136,512]{2,1,0:T(8,128)S(1)}, u32[]{:S(2)}, u32[]{:S(2)}) collective-permute-start(f32[2,136,512]{2,1,0:T(8,128)} %shard_map.109.own_ref), channel_id=1, source_target_pairs={{1,0},{2,1},{3,2},{4,3},{5,4},{6,5},{7,6},{9,8},{10,9},{11,10},{12... | collective-permute-start | bytes 1671176 | tf_op jit(solution)/shard_map/ppermute | solution.py:298
  4.6 29.3 %collective-permute-start = (f32[2,136,512]{2,1,0:T(8,128)}, f32[2,136,512]{2,1,0:T(8,128)S(1)}, u32[]{:S(2)}, u32[]{:S(2)}) collective-permute-start(f32[2,136,512]{2,1,0:T(8,128)} %shard_map.109.own_ref), channel_id=1, source_target_pairs={{0,1},{1,2},{2,3},{3,4},{4,5},{5,6},{6,7},{8,9},{9,10},{10,11},{11... | collective-permute-start | bytes 1671176 | tf_op jit(solution)/shard_map/ppermute | solution.py:298
  11.2 22.7 %copy-start = (f32[2,136,512]{2,1,0:T(8,128)S(1)}, f32[2,136,512]{2,1,0:T(8,128)}, u32[]{:S(2)}) copy-start(f32[2,136,512]{2,1,0:T(8,128)} %shard_map.109.own_ref) | copy-start | bytes 1671172
  34.0 28.4 %copy-start.1 = (f32[128,512]{1,0:T(8,128)S(1)}, f32[128,512]{1,0:T(8,128)}, u32[]{:S(2)}) copy-start(f32[128,512]{1,0:T(8,128)} %shard_map.110.heat0_ref) | copy-start | bytes 786436
  34.0 28.3 %collective-permute-start.2 = (f32[4,136,128]{2,1,0:T(8,128)S(1)}, f32[4,136,128]{2,1,0:T(8,128)S(1)}, u32[]{:S(2)}, u32[]{:S(2)}) collective-permute-start(f32[4,136,128]{2,1,0:T(8,128)S(1)} %get-tuple-element.13), channel_id=1, source_target_pairs={{0,8},{8,16},{16,24},{24,32},{32,40},{40,48},{48,56},{56,64},{64,7... | collective-permute-start | bytes 835592 | tf_op jit(solution)/shard_map/ppermute | solution.py:298
  34.8 27.5 %collective-permute-start.3 = (f32[4,136,128]{2,1,0:T(8,128)S(1)}, f32[4,136,128]{2,1,0:T(8,128)S(1)}, u32[]{:S(2)}, u32[]{:S(2)}) collective-permute-start(f32[4,136,128]{2,1,0:T(8,128)S(1)} %get-tuple-element.14), channel_id=1, source_target_pairs={{0,248},{8,0},{16,8},{24,16},{32,24},{40,32},{48,40},{56,48},{64,5... | collective-permute-start | bytes 835592 | tf_op jit(solution)/shard_map/ppermute | solution.py:298
  62.4 1.0 %copy-start.2 = (f32[128,512]{1,0:T(8,128)S(1)}, f32[128,512]{1,0:T(8,128)}, u32[]{:S(2)}) copy-start(f32[128,512]{1,0:T(8,128)} %shard_map.111.heat1_ref) | copy-start | bytes 786436

commit v5 on v4

--- a/solution.py
+++ b/solution.py
@@ -17,7 +17,7 @@
 TILE = 256
 ROWS = 8
 LANES = 128
-TOGETHER = 4
+TOGETHER = 8
 HALO = 128
 ROWS_OF_LAT, HALVES = 2, 2
 MIB = 1024 * 1024
@@ -46,9 +46,10 @@
     return lax.dot_general(left, right, (((1,), (1,)), ((), ())), preferred_element_type=jnp.float32)
 
 
-def rad_kernel(row, tally_ref, gas_hbm, mass_hbm, cos_ref, alb_ref, order_ref, table_ref, light_ref, out_ref,
+def rad_kernel(row, tally_ref, gas_hbm, mass_hbm, cos_hbm, alb_hbm, order_hbm, table_hbm, light_hbm, out_ref,
                lhs_ref, slope_ref, down_ref, up_ref, weight_ref, part_a, part_b, net_ref, whole_ref, light_log_ref, listed_ref,
-               gas_ref, mass_ref, gas_sem, mass_sem):
+               gas_ref, mass_ref, gas_sem, mass_sem,
+               cos_ref, alb_ref, order_ref, table_ref, light_ref, small_sem):
     width = 2 * TILE
 
     def copies(half):
@@ -58,9 +59,20 @@
             pltpu.make_async_copy(mass_hbm.at[row, cols], mass_ref.at[cols], mass_sem.at[half]),
         )
 
+    small = [
+        pltpu.make_async_copy(source, target, small_sem.at[k])
+        for k, (source, target) in enumerate((
+            (table_hbm, table_ref), (light_hbm, light_ref), (order_hbm, order_ref),
+            (cos_hbm, cos_ref), (alb_hbm, alb_ref),
+        ))
+    ]
+    for copy in small:
+        copy.start()
     for half in range(HALVES):
         for copy in copies(half):
             copy.start()
+    for copy in small:
+        copy.wait()
     table = table_ref[...] * DIFFUSE
     table = jnp.concatenate([table, jnp.zeros((TERMS, 256 - POINTS), jnp.float32)], axis=1)
     stacked = jnp.concatenate([table] * RUN, axis=0).T[:POINTS]
@@ -177,7 +189,7 @@
             pl.BlockSpec(memory_space=pltpu.SMEM),
             pl.BlockSpec(memory_space=pltpu.HBM),
             pl.BlockSpec(memory_space=pltpu.HBM),
-            whole((n, width)), whole((n, width)), whole((1, 256)), whole((TERMS, POINTS)), whole((1, POINTS)),
+            *[pl.BlockSpec(memory_space=pltpu.HBM)] * 5,
         ],
         out_specs=whole((TIERS, width)),
         scratch_shapes=[
@@ -196,6 +208,12 @@
             pltpu.VMEM((width, TIERS), jnp.bfloat16),
             pltpu.SemaphoreType.DMA((HALVES,)),
             pltpu.SemaphoreType.DMA((HALVES,)),
+            pltpu.VMEM((n, width), jnp.bfloat16),
+            pltpu.VMEM((n, width), jnp.bfloat16),
+            pltpu.VMEM((1, 256), jnp.int32),
+            pltpu.VMEM((TERMS, POINTS), jnp.float32),
+            pltpu.VMEM((1, POINTS), jnp.float32),
+            pltpu.SemaphoreType.DMA((5,)),
         ],
         compiler_params=pltpu.CompilerParams(vmem_limit_bytes=60 * MIB),
         cost_estimate=pl.CostEstimate(flops=2 * 10 ** 10, bytes_accessed=6 * 10 ** 6, transcendentals=6 * 10 ** 7),

time: 66.6 us -> 65.1 us (0.977)
  Pallas kernels: 49.8 us -> 48.3 us
    pallas_call x2, Pallas kernels: 45.2 us -> 43.6 us  [radiation(): pl.pallas_call(functools.partial(rad_kernel, row), out_shape=jax.ShapeDty...]
where the time goes in v5:
time: 65.1 us; the launch traced here: 64.4 us
  Pallas kernels  48.3 us (74%)
  starting transfers between devices  14.3 us (22%)
  local copies, waits for them, and re-layouts  0.99 us (2%)
  between operations  0.78 us (1%)
    pallas_call x2, Pallas kernels, radiation(): pl.pallas_call(functools.partial(rad_kernel, row), out_shape=jax.ShapeDty...  43.6 us
    ppermute x4, starting transfers between devices, shifted(): return lax.ppermute(cells, axis, pairs)  14.3 us
    pallas_call x1, Pallas kernels, march(): pl.pallas_call(march_kernel, out_shape=jax.ShapeDtypeStruct((TIERS, ROWS_...  2.68 us
    pallas_call x1, Pallas kernels, gathered(): pl.pallas_call(gathered_kernel, out_shape=jax.ShapeDtypeStruct((ROWS_OF_L...  1.97 us
  transfers between devices with their start and end apart: 4, of which 0 were waited for; matrix products, arithmetic and copies ran while one was open for 0% of the time, Pallas kernels for 68%

profile of v5, /device:TPU:65, one launch (start us, length us, event | category | flops | bytes accessed | tf_op | source)
XLA Modules:
  0.0 64.4 jit_solution(3542419678953055213)
XLA Ops:
  0.0 2.0 %shard_map.109.own_ref = f32[2,136,512]{2,1,0:T(8,128)} custom-call(f32[128,2,512]{2,1,0:T(2,128)} %field_ref.1, f32[2,2,512]{2,1,0:T(2,128)} %zonal_ref.1, f32[2,2,512]{2,1,0:T(2,128)} %meridional_ref.1), custom_call_target="tpu_custom_call" | custom-call | tf_op jit(solution)/shard_map/pallas_call | solution.py:244
  2.0 2.6 %collective-permute-start.1 = (f32[2,136,512]{2,1,0:T(8,128)}, f32[2,136,512]{2,1,0:T(8,128)S(1)}, u32[]{:S(2)}, u32[]{:S(2)}) collective-permute-start(f32[2,136,512]{2,1,0:T(8,128)} %shard_map.109.own_ref), channel_id=1, source_target_pairs={{1,0},{2,1},{3,2},{4,3},{5,4},{6,5},{7,6},{9,8},{10,9},{11,10},{12... | collective-permute-start | bytes 1671176 | tf_op jit(solution)/shard_map/ppermute | solution.py:316
  4.6 6.0 %collective-permute-start = (f32[2,136,512]{2,1,0:T(8,128)}, f32[2,136,512]{2,1,0:T(8,128)S(1)}, u32[]{:S(2)}, u32[]{:S(2)}) collective-permute-start(f32[2,136,512]{2,1,0:T(8,128)} %shard_map.109.own_ref), channel_id=1, source_target_pairs={{0,1},{1,2},{2,3},{3,4},{4,5},{5,6},{6,7},{8,9},{9,10},{10,11},{11... | collective-permute-start | bytes 1671176 | tf_op jit(solution)/shard_map/ppermute | solution.py:316
  11.2 0.0 copy-start
  11.2 21.8 %shard_map.110.heat0_ref = f32[128,512]{1,0:T(8,128)} custom-call(s32[1,1]{1,0:T(1,128)S(6)} %copy.12.tally_ref, bf16[2,512,2048]{2,1,0:T(8,128)(2,1)} %gas_hbm.2, bf16[2,512,128]{2,1,0:T(8,128)(2,1)} %mass_hbm.3, bf16[2,512]{1,0:T(2,128)(2,1)} %cos_hbm.3, bf16[2,512]{1,0:T(2,128)(2,1)} %alb_hbm.3, s32[1,256]{1,0:T(1,128)} %bitcast.2, f32[16,224]{1,0:T(8,128)} %table_hbm.3, ...), custom_call_target="tpu_custom_call" | custom-call | flops 20000000000 | bytes 6000000 | tf_op jit(solution)/shard_map/pallas_call | solution.py:185
  33.1 0.0 collective-permute-done.1.north_ref
  33.1 0.0 collective-permute-done.south_ref
  33.1 0.0 copy-done
  33.2 0.0 copy-start.1
  33.2 0.8 %collective-permute-start.2 = (f32[4,136,128]{2,1,0:T(8,128)S(1)}, f32[4,136,128]{2,1,0:T(8,128)S(1)}, u32[]{:S(2)}, u32[]{:S(2)}) collective-permute-start(f32[4,136,128]{2,1,0:T(8,128)S(1)} %get-tuple-element.13), channel_id=1, source_target_pairs={{0,8},{8,16},{16,24},{24,32},{32,40},{40,48},{48,56},{56,64},{64,7... | collective-permute-start | bytes 835592 | tf_op jit(solution)/shard_map/ppermute | solution.py:316
  34.0 4.9 %collective-permute-start.3 = (f32[4,136,128]{2,1,0:T(8,128)S(1)}, f32[4,136,128]{2,1,0:T(8,128)S(1)}, u32[]{:S(2)}, u32[]{:S(2)}) collective-permute-start(f32[4,136,128]{2,1,0:T(8,128)S(1)} %get-tuple-element.14), channel_id=1, source_target_pairs={{0,248},{8,0},{16,8},{24,16},{32,24},{40,32},{48,40},{56,48},{64,5... | collective-permute-start | bytes 835592 | tf_op jit(solution)/shard_map/ppermute | solution.py:316
  39.0 21.8 %shard_map.111.heat1_ref = f32[128,512]{1,0:T(8,128)} custom-call(s32[1,1]{1,0:T(1,128)S(6)} %copy.12.tally_ref, bf16[2,512,2048]{2,1,0:T(8,128)(2,1)} %gas_hbm.2, bf16[2,512,128]{2,1,0:T(8,128)(2,1)} %mass_hbm.3, bf16[2,512]{1,0:T(2,128)(2,1)} %cos_hbm.3, bf16[2,512]{1,0:T(2,128)(2,1)} %alb_hbm.3, s32[1,256]{1,0:T(1,128)} %bitcast.3, f32[16,224]{1,0:T(8,128)} %table_hbm.3, ...), custom_call_target="tpu_custom_call" | custom-call | flops 20000000000 | bytes 6000000 | tf_op jit(solution)/shard_map/pallas_call | solution.py:185
  60.7 0.0 collective-permute-done.2.west_ref
  60.8 0.0 collective-permute-done.3.east_ref
  60.8 0.0 copy-done.1
  60.8 0.0 copy-start.2
  60.8 0.9 %copy-done.2 = f32[128,512]{1,0:T(8,128)S(1)} copy-done((f32[128,512]{1,0:T(8,128)S(1)}, f32[128,512]{1,0:T(8,128)}, u32[]{:S(2)}) %copy-start.2) | copy-done | bytes 262168
  61.7 2.7 %shard_map.112 = f32[128,2,512]{2,1,0:T(2,128)} custom-call(f32[2,136,512]{2,1,0:T(8,128)S(1)} %copy-done, f32[2,136,512]{2,1,0:T(8,128)S(1)} %collective-permute-done.south_ref, f32[2,136,512]{2,1,0:T(8,128)S(1)} %collective-permute-done.1.north_ref, f32[4,136,128]{2,1,0:T(8,128)S(1)} %collective-permute-done.2.west_ref, ...), custom_call_target="tpu_custom_call" | custom-call | tf_op jit(solution)/shard_map/pallas_call | solution.py:306
  (3 shorter events, 0.1 us)
Async XLA Ops:
  2.0 31.1 %collective-permute-start.1 = (f32[2,136,512]{2,1,0:T(8,128)}, f32[2,136,512]{2,1,0:T(8,128)S(1)}, u32[]{:S(2)}, u32[]{:S(2)}) collective-permute-start(f32[2,136,512]{2,1,0:T(8,128)} %shard_map.109.own_ref), channel_id=1, source_target_pairs={{1,0},{2,1},{3,2},{4,3},{5,4},{6,5},{7,6},{9,8},{10,9},{11,10},{12... | collective-permute-start | bytes 1671176 | tf_op jit(solution)/shard_map/ppermute | solution.py:316
  4.6 28.5 %collective-permute-start = (f32[2,136,512]{2,1,0:T(8,128)}, f32[2,136,512]{2,1,0:T(8,128)S(1)}, u32[]{:S(2)}, u32[]{:S(2)}) collective-permute-start(f32[2,136,512]{2,1,0:T(8,128)} %shard_map.109.own_ref), channel_id=1, source_target_pairs={{0,1},{1,2},{2,3},{3,4},{4,5},{5,6},{6,7},{8,9},{9,10},{10,11},{11... | collective-permute-start | bytes 1671176 | tf_op jit(solution)/shard_map/ppermute | solution.py:316
  11.2 21.9 %copy-start = (f32[2,136,512]{2,1,0:T(8,128)S(1)}, f32[2,136,512]{2,1,0:T(8,128)}, u32[]{:S(2)}) copy-start(f32[2,136,512]{2,1,0:T(8,128)} %shard_map.109.own_ref) | copy-start | bytes 1671172
  33.2 27.6 %copy-start.1 = (f32[128,512]{1,0:T(8,128)S(1)}, f32[128,512]{1,0:T(8,128)}, u32[]{:S(2)}) copy-start(f32[128,512]{1,0:T(8,128)} %shard_map.110.heat0_ref) | copy-start | bytes 786436
  33.2 27.5 %collective-permute-start.2 = (f32[4,136,128]{2,1,0:T(8,128)S(1)}, f32[4,136,128]{2,1,0:T(8,128)S(1)}, u32[]{:S(2)}, u32[]{:S(2)}) collective-permute-start(f32[4,136,128]{2,1,0:T(8,128)S(1)} %get-tuple-element.13), channel_id=1, source_target_pairs={{0,8},{8,16},{16,24},{24,32},{32,40},{40,48},{48,56},{56,64},{64,7... | collective-permute-start | bytes 835592 | tf_op jit(solution)/shard_map/ppermute | solution.py:316
  34.0 26.7 %collective-permute-start.3 = (f32[4,136,128]{2,1,0:T(8,128)S(1)}, f32[4,136,128]{2,1,0:T(8,128)S(1)}, u32[]{:S(2)}, u32[]{:S(2)}) collective-permute-start(f32[4,136,128]{2,1,0:T(8,128)S(1)} %get-tuple-element.14), channel_id=1, source_target_pairs={{0,248},{8,0},{16,8},{24,16},{32,24},{40,32},{48,40},{56,48},{64,5... | collective-permute-start | bytes 835592 | tf_op jit(solution)/shard_map/ppermute | solution.py:316
  60.8 1.0 %copy-start.2 = (f32[128,512]{1,0:T(8,128)S(1)}, f32[128,512]{1,0:T(8,128)}, u32[]{:S(2)}) copy-start(f32[128,512]{1,0:T(8,128)} %shard_map.111.heat1_ref) | copy-start | bytes 786436
